TPU v7x, 32 devices: a whole 2x2x4 slice. The times are simulated.
32 devices in a mesh: ens: 2 (over x), lat: 16 (over z, y, core).
Axes of the slice: x: 2, y: 2, z: 4, core: 2. Of those that a mesh axis runs over, the one named last changes fastest.
Arguments:
- field_in: bfloat16 [512, 64, 1440], P('ens', 'lat'), parts along dimension 0, may hold values from -6 to 6
- filter_weight: bfloat16 [512, 9, 256], replicated, may hold values from -0.125 to 0.125
- filter_basis: bfloat16 [32, 9, 5, 33], P('lat'), may hold values from -0.71875 to 0.71875
- halo_reach: int32 [32], P('lat'), may hold values from 1 to 16, as said below
- grad_out: bfloat16 [1024, 32, 720], P('ens', 'lat'), parts along dimension 0, may hold values from -6 to 6
Outputs:
- field_out: bfloat16 [1024, 32, 720], P('ens', 'lat'), parts along dimension 0
- grad_in: bfloat16 [512, 64, 1440], P('ens', 'lat'), parts along dimension 0
- grad_weight: float32 [1024, 9, 256], P('ens'), parts along dimension 0
There are 2 independent parts, one for each index of `ens`. A program takes and returns all parts, laid end to end along the dimension named above; an argument that names none is the same for every part. Nothing has to cross between parts.
Inputs may be any that keep to these rules, and one draw needn't show every extreme that they name: `halo_reach`: some output row reaches 16.
All inputs are finite; a program needn't handle non-finite values.
Results may differ from a plain program's by a relative error of at most 0.0049.
Values may be sent and summed in bfloat16 or wider, within the bound.
A program may use at most 192 MiB of HBM per device.

v0:
```python
import functools
import math

import jax
import jax.numpy as jnp
import numpy as np
from jax import lax
from jax.experimental import pallas as pl
from jax.experimental.pallas import tpu as pltpu
from jax.sharding import PartitionSpec as P

BF16 = jnp.bfloat16
F32 = jnp.float32
OUT_BLOCK = 48
BACK_BLOCK = 32
VMEM_LIMIT = 56 * 2**20


def shifted(shard, axis, by):
    size = lax.axis_size(axis)
    pairs = [(i, i + by) for i in range(size) if 0 <= i + by < size]
    return lax.ppermute(shard, axis, pairs)


def masked_basis(filter_basis, halo_reach):
    halo = filter_basis.shape[3] // 2
    offsets = jnp.abs(lax.iota(jnp.int32, filter_basis.shape[3]) - halo)
    keep = (offsets[None, :] <= halo_reach[:, None]).astype(filter_basis.dtype)
    return filter_basis * keep[:, None, None, :]


def forward_matrix(masked):
    count, kernels, rows, taps = masked.shape
    span = 2 * OUT_BLOCK + taps - 1
    table = np.arange(span) == 2 * np.arange(OUT_BLOCK)[:, None] + np.arange(taps)[:, None, None]
    table = jnp.asarray(table.reshape(taps, -1), BF16)
    spread = jnp.dot(masked.reshape(-1, taps), table, preferred_element_type=F32).astype(BF16)
    spread = spread.reshape(count, kernels, rows, OUT_BLOCK, span).transpose(0, 1, 3, 2, 4)
    return spread.reshape(count, kernels * OUT_BLOCK, rows * span)


def backward_pairs(count, rows):
    reach = rows // 2
    return [
        (q, i + 1, q - 2 * i + reach)
        for i in range(-1, count + 1)
        for q in range(2 * count)
        if 0 <= q - 2 * i + reach < rows
    ]


def backward_matrix(masked, pairs):
    kernels, taps = masked.shape[1], masked.shape[3]
    span = BACK_BLOCK + taps // 2
    lag = np.arange(2 * BACK_BLOCK)[:, None] - 2 * np.arange(span) + taps - 1
    table = jnp.asarray((lag == np.arange(taps)[:, None, None]).reshape(taps, -1), BF16)
    picked = jnp.stack([masked[i, :, r] for _, i, r in pairs])
    spread = jnp.dot(picked.reshape(-1, taps), table, preferred_element_type=F32).astype(BF16)
    spread = spread.reshape(len(pairs), kernels, 2 * BACK_BLOCK, span).transpose(0, 2, 1, 3)
    return spread.reshape(len(pairs) * 2 * BACK_BLOCK, kernels * span)


def forward_kernel(kernels, halo, factor, own, below, above, mats, grad, inner, weight, ext):
    rows, width, chans = own.shape
    count, _, depth = mats.shape
    lat = ext.shape[0] - rows + 2
    before, after = below.shape[0], above.shape[0]
    ext[:before, halo : halo + width] = below[...]
    ext[before : before + rows, halo : halo + width] = own[...]
    ext[before + rows :, halo : halo + width] = above[...]
    ext[:, :halo] = ext[:, width : width + halo]
    ext[:, halo + width :] = ext[:, halo : 2 * halo]
    out_width = width // 2
    span = depth // lat

    for i in range(count):

        def block(b, carry, i=i):
            start = pl.multiple_of(b * 2 * OUT_BLOCK, 32)
            window = ext[2 * i : 2 * i + lat, pl.ds(start, span), :].reshape(depth, chans)
            got = jnp.dot(mats[i], window, preferred_element_type=F32).astype(BF16)
            to = pl.multiple_of(i * out_width + b * OUT_BLOCK, 16)
            for k in range(kernels):
                piece = got[k * OUT_BLOCK : (k + 1) * OUT_BLOCK]
                inner[pl.ds(to, OUT_BLOCK), k * chans : (k + 1) * chans] = piece
            return carry

        lax.fori_loop(0, out_width // OUT_BLOCK, block, 0)

    def column(k, carry):
        at = pl.ds(pl.multiple_of(k * chans, chans), chans)
        weight[:, at] = jnp.dot(grad[...], inner[:, at], preferred_element_type=F32) * factor
        return carry

    lax.fori_loop(0, kernels, column, 0)


def mix_kernel(mixer, inner, out):
    total = inner.shape[0]
    for at in range(0, total, 256):
        to = min(at + 256, total)
        got = lax.dot_general(
            mixer[...], inner[at:to], (((1,), (1,)), ((), ())), preferred_element_type=F32
        )
        out[:, at:to] = got.astype(BF16)


def backward_kernel(kernels, pairs, grads, mixer, mats, out, held):
    nrows, length, _ = grads.shape
    chans = mixer.shape[1] // kernels
    span = mats.shape[1] // kernels
    step = 2 * BACK_BLOCK
    for i in range(nrows):

        def column(k, carry, i=i):
            at = pl.ds(pl.multiple_of(k * chans, chans), chans)
            got = jnp.dot(grads[i], mixer[:, at], preferred_element_type=F32)
            held[i, :, at] = got.astype(BF16)
            return carry

        lax.fori_loop(0, kernels, column, 0)

    def block(b, carry):
        start = pl.multiple_of(b * BACK_BLOCK, 16)
        sums = [None] * out.shape[0]
        for i in range(nrows):
            mine = [n for n, p in enumerate(pairs) if p[1] == i]
            window = jnp.concatenate(
                [held[i, pl.ds(start, span), k * chans : (k + 1) * chans] for k in range(kernels)], 0
            )
            left = mats[mine[0] * step : (mine[-1] + 1) * step]
            got = jnp.dot(left, window, preferred_element_type=F32)
            for n, m in enumerate(mine):
                q = pairs[m][0]
                term = got[n * step : (n + 1) * step]
                sums[q] = term if sums[q] is None else sums[q] + term
        for q, value in enumerate(sums):
            out[q, pl.ds(pl.multiple_of(b * step, 32), step), :] = value.astype(BF16)
        return carry

    lax.fori_loop(0, out.shape[1] // step, block, 0)


def call(body, out_shape, scratch, flops, *args):
    n_bytes = sum(a.size * a.dtype.itemsize for a in args)
    whole = pl.BlockSpec(memory_space=pltpu.VMEM)
    return pl.pallas_call(
        body,
        out_shape=out_shape,
        in_specs=[whole] * len(args),
        out_specs=jax.tree.map(lambda _: whole, out_shape),
        scratch_shapes=scratch,
        compiler_params=pltpu.CompilerParams(vmem_limit_bytes=VMEM_LIMIT),
        cost_estimate=pl.CostEstimate(flops=flops, bytes_accessed=n_bytes, transcendentals=0),
    )(*args)


def summed(term, axis):
    size = lax.axis_size(axis)
    steps = size.bit_length() - 1
    if size != 1 << steps or term.shape[0] % size:
        return lax.psum(term, axis)
    me = lax.axis_index(axis)
    for bit in range(steps):
        half = term.shape[0] // 2
        pairs = [(i, i ^ (1 << bit)) for i in range(size)]
        high = (me >> bit) & 1
        sent = lax.dynamic_slice_in_dim(term, (1 - high) * half, half, 0).astype(BF16)
        kept = lax.dynamic_slice_in_dim(term, high * half, half, 0)
        term = kept + lax.ppermute(sent, axis, pairs).astype(F32)
    held = term.astype(BF16)
    for bit in reversed(range(steps)):
        pairs = [(i, i ^ (1 << bit)) for i in range(size)]
        high = ((me >> bit) & 1) == 1
        other = lax.ppermute(held, axis, pairs)
        held = jnp.concatenate(
            [jnp.where(high, other, held), jnp.where(high, held, other)], 0
        )
    return held.astype(F32)


def on_device(field_in, filter_weight, filter_basis, halo_reach, grad_out):
    chans, rows_own, width = field_in.shape
    outs, kernels, _ = filter_weight.shape
    count, out_width = grad_out.shape[1:]
    lat, taps = filter_basis.shape[2:]
    halo = taps // 2
    sds = jax.ShapeDtypeStruct

    own = field_in.transpose(1, 2, 0)
    below = shifted(own[rows_own - 2 :], "lat", 1)
    above = shifted(own[:1], "lat", -1)
    grads = grad_out.transpose(1, 2, 0)
    grad_below = shifted(grads[count - 1 :], "lat", 1)
    grad_above = shifted(grads[:1], "lat", -1)
    masked = masked_basis(filter_basis, halo_reach)
    masked_below = shifted(masked[count - 1 :], "lat", 1)
    masked_above = shifted(masked[:1], "lat", -1)
    mixer = filter_weight.reshape(outs, kernels * chans)

    factor = 1.0 / math.sqrt(lax.axis_size("lat") * count * out_width)
    total = count * out_width
    inner, weight_term = call(
        functools.partial(forward_kernel, kernels, halo, factor),
        (sds((total, kernels * chans), BF16), sds((outs, kernels * chans), F32)),
        [pltpu.VMEM((rows_own + 3, width + 2 * halo, chans), BF16)],
        10**10,
        own,
        below,
        above,
        forward_matrix(masked),
        grad_out.reshape(outs, total),
    )
    grad_weight = summed(weight_term, "lat").reshape(outs, kernels, chans)

    field_out = call(mix_kernel, sds((outs, total), BF16), [], 4 * 10**9, mixer, inner)
    field_out = field_out.reshape(outs, count, out_width)

    pairs = backward_pairs(count, lat)
    blocks = -(-out_width // BACK_BLOCK)
    span = BACK_BLOCK + halo
    length = (blocks - 1) * BACK_BLOCK + span
    lead = halo // 2
    all_grads = jnp.concatenate([grad_below, grads, grad_above], 0)
    all_grads = jnp.concatenate(
        [all_grads[:, out_width - lead :], all_grads, all_grads[:, : length - lead - out_width]], 1
    )
    all_masked = jnp.concatenate([masked_below, masked, masked_above], 0)
    back = call(
        functools.partial(backward_kernel, kernels, pairs),
        sds((rows_own, blocks * 2 * BACK_BLOCK, chans), BF16),
        [pltpu.VMEM((count + 2, length, kernels * chans), BF16)],
        14 * 10**9,
        all_grads,
        mixer,
        backward_matrix(all_masked, pairs),
    )
    grad_in = back[:, :width].transpose(2, 0, 1)
    return (field_out, grad_in, grad_weight)


def solution(mesh):
    return jax.shard_map(
        on_device,
        mesh=mesh,
        in_specs=(
            P("ens", "lat", None),
            P(),
            P("lat", None, None, None),
            P("lat"),
            P("ens", "lat", None),
        ),
        out_specs=(P("ens", "lat", None), P("ens", "lat", None), P("ens", None, None)),
        check_vma=False,
    )
```

profile of v0, /device:TPU:0, one launch (start us, length us, event | category | flops | bytes accessed | tf_op | source)
XLA Modules:
  0.0 208.4 jit_solution(17264719864531060721)
XLA Ops:
  0.6 0.0 copy-start.5
  0.7 2.6 %slice.76 = bf16[2,1440,256]{2,1,0:T(8,128)(2,1)} slice(bf16[4,1440,256]{2,1,0:T(8,128)(2,1)} %bitcast.72), slice={[2:4], [0:1440], [0:256]} | slice | bytes 2949120 | tf_op jit(solution)/shard_map/slice | solution.py:191
  3.3 3.5 %collective-permute-start = (bf16[2,1440,256]{2,1,0:T(8,128)(2,1)}, bf16[2,1440,256]{2,1,0:T(8,128)(2,1)}, u32[]{:S(2)}, u32[]{:S(2)}) collective-permute-start(bf16[2,1440,256]{2,1,0:T(8,128)(2,1)} %slice.76), channel_id=1, source_target_pairs={{0,1},{1,2},{2,3},{3,4},{4,5},{5,6},{6,7},{7,8},{8,9},{9,10},{10,1... | collective-permute-start | bytes 4423688 | tf_op jit(solution)/shard_map/ppermute | solution.py:22
  6.8 2.0 slice.77
  8.8 1.3 collective-permute-start.1
  10.1 0.1 compare_convert_fusion
  10.3 0.5 convolution_convert_fusion
  10.8 0.2 copy.41
  11.0 0.1 slice.93
  11.1 0.0 copy-start
  11.1 0.5 copy.44
  11.5 2.2 %reshape.68.mats = bf16[2,432,640]{2,1,0:T(8,128)(2,1)} reshape(bf16[2,9,48,5,128]{4,3,2,1,0:T(8,128)(2,1)S(1)} %bitcast.65) | data formatting | bytes 2211840 | tf_op jit(solution)/shard_map/reshape | solution.py:39
  13.7 1.6 copy.30.grad
  15.3 0.0 collective-permute-done.1.above
  15.3 0.0 collective-permute-done.below
  15.3 22.9 %shard_map.94 = (bf16[1440,2304]{1,0:T(8,128)(2,1)}, f32[512,2304]{1,0:T(8,128)}) custom-call(bf16[4,1440,256]{2,1,0:T(8,128)(2,1)} %bitcast.74, bf16[2,1440,256]{2,1,0:T(8,128)(2,1)} %collective-permute-done.below, bf16[1,1440,256]{2,1,0:T(8,128)(2,1)} %collective-permute-done.1.above, bf16[2,432,640]{2,1,0:T(8,128)(2,1)} %reshape.68.mats, ...), custom_call_target="tpu_custom_call" | custom-call | flops 10000000000 | bytes 7741440 | tf_op jit(solution)/shard_map/pallas_call | solution.py:147
  38.2 1.8 dynamic-slice_convert_fusion
  40.0 17.6 %collective-permute-start.6 = (bf16[256,2304]{1,0:T(8,128)(2,1)S(1)}, bf16[256,2304]{1,0:T(8,128)(2,1)}, u32[]{:S(2)}, u32[]{:S(2)}) collective-permute-start(bf16[256,2304]{1,0:T(8,128)(2,1)S(1)} %dynamic-slice_convert_fusion), channel_id=1, source_target_pairs={{0,1},{1,0},{2,3},{3,2},{4,5},{5,4},{6,7},{7,6},{8,9},{9,8},{10,11... | collective-permute-start | bytes 3538952 | tf_op jit(solution)/shard_map/ppermute | solution.py:170
  57.6 1.9 collective-permute-start.4
  59.5 1.3 fusion.2
  60.8 1.3 collective-permute-start.3
  62.1 5.9 %collective-permute-start.2 = (bf16[1,720,512]{2,1,0:T(8,128)(2,1)}, bf16[1,720,512]{2,1,0:T(8,128)(2,1)}, u32[]{:S(2)}, u32[]{:S(2)}) collective-permute-start(bf16[1,720,512]{2,1,0:T(8,128)(2,1)} %get-tuple-element.15), channel_id=1, source_target_pairs={{0,1},{1,2},{2,3},{3,4},{4,5},{5,6},{6,7},{7,8},{8,9},{9,10},{10,1... | collective-permute-start | bytes 2211848 | tf_op jit(solution)/shard_map/ppermute | solution.py:22
  68.0 1.5 collective-permute-start.5
  69.5 4.3 %copy.26 = bf16[512,9,256]{0,2,1:T(8,128)(2,1)} copy(bf16[512,9,256]{2,0,1:T(8,128)(2,1)} %param.8) | data formatting | bytes 4718592 | tf_op args[1]
  73.8 4.3 %copy.31.mixer = bf16[512,2304]{1,0:T(8,128)(2,1)} copy(bf16[512,2304]{0,1:T(8,128)(2,1)} %bitcast.64) | data formatting | bytes 4718592 | tf_op jit(solution)/shard_map/reshape | solution.py:199
  78.1 0.0 collective-permute-done.4
  78.1 0.0 collective-permute-done.6
  78.1 2.2 %convert_add_fusion = f32[256,2304]{1,0:T(8,128)S(1)} fusion(bf16[256,2304]{1,0:T(8,128)(2,1)} %collective-permute-done.6, f32[512,2304]{1,0:T(8,128)} %get-tuple-element.6, s32[]{:T(128)S(6)} %select_n.76), kind=kLoop, calls=%fused_computation.10 | loop fusion | flops 1179648 | bytes 5898244 | tf_op jit(solution)/shard_map/add | solution.py:170
  80.4 0.1 dynamic-slice_convert_fusion.1
  80.5 3.2 %collective-permute-start.7 = (bf16[128,2304]{1,0:T(8,128)(2,1)S(1)}, bf16[128,2304]{1,0:T(8,128)(2,1)S(1)}, u32[]{:S(2)}, u32[]{:S(2)}) collective-permute-start(bf16[128,2304]{1,0:T(8,128)(2,1)S(1)} %dynamic-slice_convert_fusion.1), channel_id=1, source_target_pairs={{0,2},{1,3},{2,0},{3,1},{4,6},{5,7},{6,4},{7,5},{8,10},{9,11},{10,... | collective-permute-start | bytes 1769480 | tf_op jit(solution)/shard_map/ppermute | solution.py:170
  83.6 13.8 %collective-permute-done.7 = bf16[128,2304]{1,0:T(8,128)(2,1)S(1)} collective-permute-done((bf16[128,2304]{1,0:T(8,128)(2,1)S(1)}, bf16[128,2304]{1,0:T(8,128)(2,1)S(1)}, u32[]{:S(2)}, u32[]{:S(2)}) %collective-permute-start.7) | collective-permute-done | bytes 589856 | tf_op jit(solution)/shard_map/ppermute | solution.py:170
  97.4 0.1 convert_add_fusion.1
  97.5 0.0 copy-start.6
  97.6 2.8 %collective-permute-start.8 = (bf16[64,2304]{1,0:T(8,128)(2,1)S(1)}, bf16[64,2304]{1,0:T(8,128)(2,1)S(1)}, u32[]{:S(2)}, u32[]{:S(2)}) collective-permute-start(bf16[64,2304]{1,0:T(8,128)(2,1)S(1)} %dynamic-slice_convert_fusion.2), channel_id=1, source_target_pairs={{0,4},{1,5},{2,6},{3,7},{4,0},{5,1},{6,2},{7,3},{8,12},{9,13},{10,... | collective-permute-start | bytes 884744 | tf_op jit(solution)/shard_map/ppermute | solution.py:170
  100.4 6.7 %collective-permute-done.8 = bf16[64,2304]{1,0:T(8,128)(2,1)S(1)} collective-permute-done((bf16[64,2304]{1,0:T(8,128)(2,1)S(1)}, bf16[64,2304]{1,0:T(8,128)(2,1)S(1)}, u32[]{:S(2)}, u32[]{:S(2)}) %collective-permute-start.8) | collective-permute-done | bytes 294944 | tf_op jit(solution)/shard_map/ppermute | solution.py:170
  107.1 0.1 convert_add_fusion.2
  107.2 2.3 %collective-permute-start.9 = (bf16[32,2304]{1,0:T(8,128)(2,1)S(1)}, bf16[32,2304]{1,0:T(8,128)(2,1)S(1)}, u32[]{:S(2)}, u32[]{:S(2)}) collective-permute-start(bf16[32,2304]{1,0:T(8,128)(2,1)S(1)} %dynamic-slice_convert_fusion.3), channel_id=1, source_target_pairs={{0,8},{1,9},{2,10},{3,11},{4,12},{5,13},{6,14},{7,15},{8,0},{9,1},... | collective-permute-start | bytes 442376 | tf_op jit(solution)/shard_map/ppermute | solution.py:170
  109.5 7.9 %collective-permute-done.9 = bf16[32,2304]{1,0:T(8,128)(2,1)S(1)} collective-permute-done((bf16[32,2304]{1,0:T(8,128)(2,1)S(1)}, bf16[32,2304]{1,0:T(8,128)(2,1)S(1)}, u32[]{:S(2)}, u32[]{:S(2)}) %collective-permute-start.9) | collective-permute-done | bytes 147488 | tf_op jit(solution)/shard_map/ppermute | solution.py:170
  117.4 0.1 collective-permute-start.10
  117.5 0.0 collective-permute-done.5
  117.5 6.0 %collective-permute-done.10 = bf16[32,2304]{1,0:T(8,128)(2,1)S(1)} collective-permute-done((bf16[32,2304]{1,0:T(8,128)(2,1)S(1)}, bf16[32,2304]{1,0:T(8,128)(2,1)S(1)}, u32[]{:S(2)}, u32[]{:S(2)}) %collective-permute-start.10) | collective-permute-done | bytes 147488 | tf_op jit(solution)/shard_map/ppermute | solution.py:175
  123.6 0.6 copy-done.1
  124.2 0.7 pad_maximum_fusion.6
  125.0 0.3 convolution_convert_fusion.1
  125.3 1.5 reshape.72
  126.8 2.8 %copy.39 = bf16[10,64,9,48]{3,2,1,0:T(8,128)(2,1)} copy(bf16[10,64,9,48]{3,1,2,0:T(8,128)(2,1)S(1)} %bitcast.66) | data formatting | bytes 1105920 | tf_op jit(solution)/shard_map/reshape | solution.py:60
  129.6 4.3 %reshape.74.mats = bf16[640,432]{1,0:T(8,128)(2,1)} reshape(bf16[10,64,9,48]{3,2,1,0:T(8,128)(2,1)} %copy.39) | data formatting | bytes 1105920 | tf_op jit(solution)/shard_map/reshape | solution.py:60
  133.9 0.0 collective-permute-done.11
  133.9 1.1 broadcast_select_fusion.5
  135.0 3.8 %collective-permute-start.12 = (bf16[128,2304]{1,0:T(8,128)(2,1)S(1)}, bf16[128,2304]{1,0:T(8,128)(2,1)S(1)}, u32[]{:S(2)}, u32[]{:S(2)}) collective-permute-start(bf16[128,2304]{1,0:T(8,128)(2,1)S(1)} %pad_maximum_fusion.5), channel_id=1, source_target_pairs={{0,2},{1,3},{2,0},{3,1},{4,6},{5,7},{6,4},{7,5},{8,10},{9,11},{10,... | collective-permute-start | bytes 1769480 | tf_op jit(solution)/shard_map/ppermute | solution.py:175
  138.9 2.9 %fusion.grads = bf16[4,752,512]{2,1,0:T(8,128)(2,1)} fusion(bf16[1,720,512]{2,1,0:T(8,128)(2,1)} %collective-permute-done.3, bf16[2,720,512]{2,1,0:T(8,128)(2,1)S(1)} %bitcast.63, bf16[1,720,512]{2,1,0:T(8,128)(2,1)} %collective-permute-done.2), kind=kLoop, calls=%fused_computation.3 | loop fusion | flops 27721728 | bytes 6029312 | tf_op jit(solution)/shard_map/concatenate | solution.py:225
  141.8 10.3 %collective-permute-done.12 = bf16[128,2304]{1,0:T(8,128)(2,1)S(1)} collective-permute-done((bf16[128,2304]{1,0:T(8,128)(2,1)S(1)}, bf16[128,2304]{1,0:T(8,128)(2,1)S(1)}, u32[]{:S(2)}, u32[]{:S(2)}) %collective-permute-start.12) | collective-permute-done | bytes 589856 | tf_op jit(solution)/shard_map/ppermute | solution.py:175
  152.1 0.2 broadcast_select_fusion.3
  152.3 0.1 pad_maximum_fusion.4
  152.4 0.1 collective-permute-start.13
  152.5 25.4 %shard_map.96 = bf16[4,1472,256]{2,1,0:T(8,128)(2,1)} custom-call(bf16[4,752,512]{2,1,0:T(8,128)(2,1)} %fusion.grads, bf16[512,2304]{1,0:T(8,128)(2,1)} %copy.31.mixer, bf16[640,432]{1,0:T(8,128)(2,1)} %reshape.74.mats), custom_call_target="tpu_custom_call" | custom-call | flops 14000000000 | bytes 5992448 | tf_op jit(solution)/shard_map/pallas_call | solution.py:147
  177.9 3.6 %slice_bitcast_fusion = bf16[256,4,1440]{0,2,1:T(8,128)(2,1)} fusion(bf16[4,1472,256]{2,1,0:T(8,128)(2,1)} %shard_map.96), kind=kLoop, calls=%fused_computation.8 | loop fusion | bytes 5898240 | tf_op jit(solution)/shard_map/transpose | solution.py:238
  181.5 8.6 %shard_map.95 = bf16[512,1440]{1,0:T(8,128)(2,1)} custom-call(bf16[512,2304]{1,0:T(8,128)(2,1)} %copy.31.mixer, bf16[1440,2304]{1,0:T(8,128)(2,1)} %get-tuple-element.5.inner), custom_call_target="tpu_custom_call" | custom-call | flops 4000000000 | bytes 8994816 | tf_op jit(solution)/shard_map/pallas_call | solution.py:147
  190.1 2.6 %copy.32 = bf16[512,1440]{0,1:T(8,128)(2,1)} copy(bf16[512,1440]{1,0:T(8,128)(2,1)} %shard_map.95) | data formatting | bytes 2949120 | tf_op jit(solution)/shard_map/pallas_call | solution.py:147
  192.7 2.7 %broadcast_select_fusion.1 = (bf16[256,2304]{1,0:T(8,128)(2,1)S(1)}, bf16[256,2304]{1,0:T(8,128)(2,1)}) fusion(bf16[256,2304]{1,0:T(8,128)(2,1)} %collective-permute-done.13, pred[]{:T(512)S(6)} %eq.12, bf16[128,2304]{1,0:T(8,128)(2,1)S(1)} %get-tuple-element.18, bf16[128,2304]{1,0:T(8,128)(2,1)S(1)} %get-tuple-element.17), kind=kLoop, calls=%fused_computation.17 | loop fusion | flops 3538944 | bytes 4718593 | tf_op jit(solution)/shard_map/jit(_where)/select_n | solution.py:177
  195.3 1.6 copy.37
  196.9 1.4 copy.36
  198.3 4.1 %maximum_convert_fusion = f32[512,9,256]{0,2,1:T(8,128)} fusion(bf16[256,9,256]{0,2,1:T(8,128)(2,1)S(1)} %bitcast.67, bf16[256,9,256]{0,2,1:T(8,128)(2,1)} %bitcast.68), kind=kLoop, calls=%fused_computation.9 | loop fusion | flops 4718592 | bytes 7077888 | tf_op jit(solution)/shard_map/convert_element_type | solution.py:179
  202.4 6.0 %copy.38 = f32[512,9,256]{2,0,1:T(8,128)} copy(f32[512,9,256]{0,2,1:T(8,128)} %maximum_convert_fusion) | data formatting | bytes 9437184
  (39 shorter events, 0.4 us)
Async XLA Ops:
  0.6 9.6 %copy-start.5 = (bf16[33,6144]{1,0:T(8,128)(2,1)S(1)}, bf16[33,6144]{1,0:T(8,128)(2,1)}, u32[]{:S(2)}) copy-start(bf16[33,6144]{1,0:T(8,128)(2,1)} %constant.29.clone) | copy-start | bytes 1216516
  0.6 9.5 %copy-start.8 = (s32[2]{0:T(128)S(1)}, s32[2]{0:T(128)}, u32[]{:S(2)}) copy-start(s32[2]{0:T(128)} %param.10) | copy-start | bytes 28
  0.7 9.6 %copy-start.7 = (bf16[2,9,5,33]{3,0,2,1:T(2,128)(2,1)S(1)}, bf16[2,9,5,33]{3,0,2,1:T(2,128)(2,1)}, u32[]{:S(2)}) copy-start(bf16[2,9,5,33]{3,0,2,1:T(2,128)(2,1)} %param.9) | copy-start | bytes 17824
  3.3 12.0 %collective-permute-start = (bf16[2,1440,256]{2,1,0:T(8,128)(2,1)}, bf16[2,1440,256]{2,1,0:T(8,128)(2,1)}, u32[]{:S(2)}, u32[]{:S(2)}) collective-permute-start(bf16[2,1440,256]{2,1,0:T(8,128)(2,1)} %slice.76), channel_id=1, source_target_pairs={{0,1},{1,2},{2,3},{3,4},{4,5},{5,6},{6,7},{7,8},{8,9},{9,10},{10,1... | collective-permute-start | bytes 4423688 | tf_op jit(solution)/shard_map/ppermute | solution.py:22
  8.8 6.4 %collective-permute-start.1 = (bf16[1,1440,256]{2,1,0:T(8,128)(2,1)}, bf16[1,1440,256]{2,1,0:T(8,128)(2,1)}, u32[]{:S(2)}, u32[]{:S(2)}) collective-permute-start(bf16[1,1440,256]{2,1,0:T(8,128)(2,1)} %slice.77), channel_id=1, source_target_pairs={{1,0},{2,1},{3,2},{4,3},{5,4},{6,5},{7,6},{8,7},{9,8},{10,9},{11,1... | collective-permute-start | bytes 2211848 | tf_op jit(solution)/shard_map/ppermute | solution.py:22
  11.1 2.6 %copy-start = (bf16[512,2,720]{0,2,1:T(8,128)(2,1)S(1)}, bf16[512,2,720]{0,2,1:T(8,128)(2,1)}, u32[]{:S(2)}) copy-start(bf16[512,2,720]{0,2,1:T(8,128)(2,1)} %param.11) | copy-start | bytes 4423684
  40.0 38.1 %collective-permute-start.6 = (bf16[256,2304]{1,0:T(8,128)(2,1)S(1)}, bf16[256,2304]{1,0:T(8,128)(2,1)}, u32[]{:S(2)}, u32[]{:S(2)}) collective-permute-start(bf16[256,2304]{1,0:T(8,128)(2,1)S(1)} %dynamic-slice_convert_fusion), channel_id=1, source_target_pairs={{0,1},{1,0},{2,3},{3,2},{4,5},{5,4},{6,7},{7,6},{8,9},{9,8},{10,11... | collective-permute-start | bytes 3538952 | tf_op jit(solution)/shard_map/ppermute | solution.py:170
  57.6 20.5 %collective-permute-start.4 = (bf16[1,9,5,33]{3,1,2,0:T(8,128)(2,1)S(1)}, bf16[1,9,5,33]{3,1,2,0:T(8,128)(2,1)S(1)}, u32[]{:S(2)}, u32[]{:S(2)}) collective-permute-start(bf16[1,9,5,33]{3,1,2,0:T(8,128)(2,1)S(1)} %get-tuple-element.24), channel_id=1, source_target_pairs={{0,1},{1,2},{2,3},{3,4},{4,5},{5,6},{6,7},{7,8},{8,9},{9,10},{10,1... | collective-permute-start | bytes 8918 | tf_op jit(solution)/shard_map/ppermute | solution.py:22
  60.8 78.1 %collective-permute-start.3 = (bf16[1,720,512]{2,1,0:T(8,128)(2,1)}, bf16[1,720,512]{2,1,0:T(8,128)(2,1)}, u32[]{:S(2)}, u32[]{:S(2)}) collective-permute-start(bf16[1,720,512]{2,1,0:T(8,128)(2,1)} %get-tuple-element.16), channel_id=1, source_target_pairs={{1,0},{2,1},{3,2},{4,3},{5,4},{6,5},{7,6},{8,7},{9,8},{10,9},{11,1... | collective-permute-start | bytes 2211848 | tf_op jit(solution)/shard_map/ppermute | solution.py:22
  62.1 76.8 %collective-permute-start.2 = (bf16[1,720,512]{2,1,0:T(8,128)(2,1)}, bf16[1,720,512]{2,1,0:T(8,128)(2,1)}, u32[]{:S(2)}, u32[]{:S(2)}) collective-permute-start(bf16[1,720,512]{2,1,0:T(8,128)(2,1)} %get-tuple-element.15), channel_id=1, source_target_pairs={{0,1},{1,2},{2,3},{3,4},{4,5},{5,6},{6,7},{7,8},{8,9},{9,10},{10,1... | collective-permute-start | bytes 2211848 | tf_op jit(solution)/shard_map/ppermute | solution.py:22
  68.0 49.5 %collective-permute-start.5 = (bf16[1,9,5,33]{3,1,2,0:T(8,128)(2,1)S(1)}, bf16[1,9,5,33]{3,1,2,0:T(8,128)(2,1)S(1)}, u32[]{:S(2)}, u32[]{:S(2)}) collective-permute-start(bf16[1,9,5,33]{3,1,2,0:T(8,128)(2,1)S(1)} %get-tuple-element.23), channel_id=1, source_target_pairs={{1,0},{2,1},{3,2},{4,3},{5,4},{6,5},{7,6},{8,7},{9,8},{10,9},{11,1... | collective-permute-start | bytes 8918 | tf_op jit(solution)/shard_map/ppermute | solution.py:22
  80.5 16.9 %collective-permute-start.7 = (bf16[128,2304]{1,0:T(8,128)(2,1)S(1)}, bf16[128,2304]{1,0:T(8,128)(2,1)S(1)}, u32[]{:S(2)}, u32[]{:S(2)}) collective-permute-start(bf16[128,2304]{1,0:T(8,128)(2,1)S(1)} %dynamic-slice_convert_fusion.1), channel_id=1, source_target_pairs={{0,2},{1,3},{2,0},{3,1},{4,6},{5,7},{6,4},{7,5},{8,10},{9,11},{10,... | collective-permute-start | bytes 1769480 | tf_op jit(solution)/shard_map/ppermute | solution.py:170
  97.5 27.5 %copy-start.6 = (bf16[33,3072]{1,0:T(8,128)(2,1)S(1)}, bf16[33,3072]{1,0:T(8,128)(2,1)}, u32[]{:S(2)}) copy-start(bf16[33,3072]{1,0:T(8,128)(2,1)} %constant.30.clone) | copy-start | bytes 608260
  97.6 9.5 %collective-permute-start.8 = (bf16[64,2304]{1,0:T(8,128)(2,1)S(1)}, bf16[64,2304]{1,0:T(8,128)(2,1)S(1)}, u32[]{:S(2)}, u32[]{:S(2)}) collective-permute-start(bf16[64,2304]{1,0:T(8,128)(2,1)S(1)} %dynamic-slice_convert_fusion.2), channel_id=1, source_target_pairs={{0,4},{1,5},{2,6},{3,7},{4,0},{5,1},{6,2},{7,3},{8,12},{9,13},{10,... | collective-permute-start | bytes 884744 | tf_op jit(solution)/shard_map/ppermute | solution.py:170
  107.2 10.2 %collective-permute-start.9 = (bf16[32,2304]{1,0:T(8,128)(2,1)S(1)}, bf16[32,2304]{1,0:T(8,128)(2,1)S(1)}, u32[]{:S(2)}, u32[]{:S(2)}) collective-permute-start(bf16[32,2304]{1,0:T(8,128)(2,1)S(1)} %dynamic-slice_convert_fusion.3), channel_id=1, source_target_pairs={{0,8},{1,9},{2,10},{3,11},{4,12},{5,13},{6,14},{7,15},{8,0},{9,1},... | collective-permute-start | bytes 442376 | tf_op jit(solution)/shard_map/ppermute | solution.py:170
  117.4 6.1 %collective-permute-start.10 = (bf16[32,2304]{1,0:T(8,128)(2,1)S(1)}, bf16[32,2304]{1,0:T(8,128)(2,1)S(1)}, u32[]{:S(2)}, u32[]{:S(2)}) collective-permute-start(bf16[32,2304]{1,0:T(8,128)(2,1)S(1)} %add_convert_fusion), channel_id=1, source_target_pairs={{0,8},{1,9},{2,10},{3,11},{4,12},{5,13},{6,14},{7,15},{8,0},{9,1},... | collective-permute-start | bytes 442376 | tf_op jit(solution)/shard_map/ppermute | solution.py:175
  123.6 0.7 copy-start.1
  123.6 1.4 copy-start.3
  125.0 9.0 %collective-permute-start.11 = (bf16[64,2304]{1,0:T(8,128)(2,1)}, bf16[64,2304]{1,0:T(8,128)(2,1)}, u32[]{:S(2)}, u32[]{:S(2)}) collective-permute-start(bf16[64,2304]{1,0:T(8,128)(2,1)} %pad_maximum_fusion.6), channel_id=1, source_target_pairs={{0,4},{1,5},{2,6},{3,7},{4,0},{5,1},{6,2},{7,3},{8,12},{9,13},{10,... | collective-permute-start | bytes 884744 | tf_op jit(solution)/shard_map/ppermute | solution.py:175
  129.6 4.3 %copy-start.2 = (bf16[32,2304]{1,0:T(8,128)(2,1)S(1)}, bf16[32,2304]{1,0:T(8,128)(2,1)}, u32[]{:S(2)}) copy-start(bf16[32,2304]{1,0:T(8,128)(2,1)} %copy-done.1) | copy-start | bytes 442372
  129.6 4.3 %copy-start.4 = (bf16[32,2304]{1,0:T(8,128)(2,1)S(1)}, bf16[32,2304]{1,0:T(8,128)(2,1)}, u32[]{:S(2)}) copy-start(bf16[32,2304]{1,0:T(8,128)(2,1)} %copy-done.3) | copy-start | bytes 442372
  135.0 17.1 %collective-permute-start.12 = (bf16[128,2304]{1,0:T(8,128)(2,1)S(1)}, bf16[128,2304]{1,0:T(8,128)(2,1)S(1)}, u32[]{:S(2)}, u32[]{:S(2)}) collective-permute-start(bf16[128,2304]{1,0:T(8,128)(2,1)S(1)} %pad_maximum_fusion.5), channel_id=1, source_target_pairs={{0,2},{1,3},{2,0},{3,1},{4,6},{5,7},{6,4},{7,5},{8,10},{9,11},{10,... | collective-permute-start | bytes 1769480 | tf_op jit(solution)/shard_map/ppermute | solution.py:175
  152.4 40.3 %collective-permute-start.13 = (bf16[256,2304]{1,0:T(8,128)(2,1)S(1)}, bf16[256,2304]{1,0:T(8,128)(2,1)}, u32[]{:S(2)}, u32[]{:S(2)}) collective-permute-start(bf16[256,2304]{1,0:T(8,128)(2,1)S(1)} %pad_maximum_fusion.4), channel_id=1, source_target_pairs={{0,1},{1,0},{2,3},{3,2},{4,5},{5,4},{6,7},{7,6},{8,9},{9,8},{10,11... | collective-permute-start | bytes 3538952 | tf_op jit(solution)/shard_map/ppermute | solution.py:175
where the time goes:
time: 209 us; the launch traced here: 208 us
  Pallas kernels  56.9 us (27%)
  local copies, waits for them, and re-layouts  45.6 us (22%)
  starting transfers between devices  45.2 us (22%)
  waiting for transfers between devices  44.7 us (21%)
  other arithmetic  14.3 us (7%)
    pallas_call x3, Pallas kernels, call(): pl.pallas_call(body, out_shape=out_shape, in_specs=[whole] * len(args), o...  56.9 us
    ppermute x4, waiting for transfers between devices, summed(): term = kept + lax.ppermute(sent, axis, pairs).astype(F32)  28.3 us
    ppermute x4, starting transfers between devices, summed(): term = kept + lax.ppermute(sent, axis, pairs).astype(F32)  25.9 us
    ppermute x4, waiting for transfers between devices, summed(): other = lax.ppermute(held, axis, pairs)  16.3 us
    ppermute x6, starting transfers between devices, shifted(): return lax.ppermute(shard, axis, pairs)  15.4 us
    unnamed x31, local copies, waits for them, and re-layouts  11.4 us
    reshape x2, local copies, waits for them, and re-layouts, backward_matrix(): return spread.reshape(len(pairs) * 2 * BACK_BLOCK, kernels * span)  7.09 us
    reshape x1, local copies, waits for them, and re-layouts, on_device(): mixer = filter_weight.reshape(outs, kernels * chans)  4.34 us
  transfers between devices with their start and end apart: 14, of which 5 were waited for; matrix products, arithmetic and copies ran while one was open for 19% of the time, Pallas kernels for 16%

commit v1 on v0

--- a/solution.py
+++ b/solution.py
@@ -13,6 +13,7 @@
 F32 = jnp.float32
 OUT_BLOCK = 48
 BACK_BLOCK = 32
+MIX_PARTS = 6
 VMEM_LIMIT = 56 * 2**20
 
 
@@ -89,38 +90,48 @@
 
     def column(k, carry):
         at = pl.ds(pl.multiple_of(k * chans, chans), chans)
-        weight[:, at] = jnp.dot(grad[...], inner[:, at], preferred_element_type=F32) * factor
+        weight[k] = jnp.dot(grad[...], inner[:, at], preferred_element_type=F32) * factor
         return carry
 
     lax.fori_loop(0, kernels, column, 0)
 
 
-def mix_kernel(mixer, inner, out):
+def mix_kernel(mixer, inner, out, wide):
+    kernels, _, chans = mixer.shape
+    for k in range(kernels):
+        wide[:, k * chans : (k + 1) * chans] = mixer[k]
     total = inner.shape[0]
-    for at in range(0, total, 256):
-        to = min(at + 256, total)
+    rows = total // MIX_PARTS
+
+    def part(n, carry):
+        at = pl.ds(pl.multiple_of(n * rows, 16), rows)
         got = lax.dot_general(
-            mixer[...], inner[at:to], (((1,), (1,)), ((), ())), preferred_element_type=F32
-        )
-        out[:, at:to] = got.astype(BF16)
+            inner[at], wide[...], (((1,), (1,)), ((), ())), preferred_element_type=F32
+        )
+        out[at] = got.astype(BF16)
+        return carry
+
+    lax.fori_loop(0, MIX_PARTS, part, 0)
 
 
 def backward_kernel(kernels, pairs, grads, mixer, mats, out, held):
     nrows, length, _ = grads.shape
-    chans = mixer.shape[1] // kernels
+    chans = mixer.shape[2]
     span = mats.shape[1] // kernels
     step = 2 * BACK_BLOCK
     for i in range(nrows):
 
         def column(k, carry, i=i):
             at = pl.ds(pl.multiple_of(k * chans, chans), chans)
-            got = jnp.dot(grads[i], mixer[:, at], preferred_element_type=F32)
+            got = jnp.dot(grads[i], mixer[k], preferred_element_type=F32)
             held[i, :, at] = got.astype(BF16)
             return carry
 
         lax.fori_loop(0, kernels, column, 0)
 
-    def block(b, carry):
+    width = out.shape[1]
+
+    def block(b, size):
         start = pl.multiple_of(b * BACK_BLOCK, 16)
         sums = [None] * out.shape[0]
         for i in range(nrows):
@@ -135,10 +146,15 @@
                 term = got[n * step : (n + 1) * step]
                 sums[q] = term if sums[q] is None else sums[q] + term
         for q, value in enumerate(sums):
-            out[q, pl.ds(pl.multiple_of(b * step, 32), step), :] = value.astype(BF16)
+            out[q, pl.ds(pl.multiple_of(b * step, 32), size), :] = value[:size].astype(BF16)
+
+    def whole_block(b, carry):
+        block(b, step)
         return carry
 
-    lax.fori_loop(0, out.shape[1] // step, block, 0)
+    lax.fori_loop(0, width // step, whole_block, 0)
+    if width % step:
+        block(width // step, width % step)
 
 
 def call(body, out_shape, scratch, flops, *args):
@@ -155,28 +171,40 @@
     )(*args)
 
 
-def summed(term, axis):
+def tied(value, *others):
+    return lax.optimization_barrier((value, *others))
+
+
+def summed(term, axis, work):
     size = lax.axis_size(axis)
     steps = size.bit_length() - 1
-    if size != 1 << steps or term.shape[0] % size:
-        return lax.psum(term, axis)
+    if size != 1 << steps or term.shape[1] % size:
+        return (lax.psum(term, axis), *(make(x) for make, x in work))
     me = lax.axis_index(axis)
+    done = []
     for bit in range(steps):
-        half = term.shape[0] // 2
+        half = term.shape[1] // 2
         pairs = [(i, i ^ (1 << bit)) for i in range(size)]
         high = (me >> bit) & 1
-        sent = lax.dynamic_slice_in_dim(term, (1 - high) * half, half, 0).astype(BF16)
-        kept = lax.dynamic_slice_in_dim(term, high * half, half, 0)
-        term = kept + lax.ppermute(sent, axis, pairs).astype(F32)
+        sent = lax.dynamic_slice_in_dim(term, (1 - high) * half, half, 1).astype(BF16)
+        kept = lax.dynamic_slice_in_dim(term, high * half, half, 1)
+        if bit > 0 and work:
+            (make, given), work = work[0], work[1:]
+            sent, given = tied(sent, given)
+            other, made = tied(lax.ppermute(sent, axis, pairs), make(given))
+            done.append(made)
+        else:
+            other = lax.ppermute(sent, axis, pairs)
+        term = kept + other.astype(F32)
     held = term.astype(BF16)
     for bit in reversed(range(steps)):
         pairs = [(i, i ^ (1 << bit)) for i in range(size)]
         high = ((me >> bit) & 1) == 1
         other = lax.ppermute(held, axis, pairs)
         held = jnp.concatenate(
-            [jnp.where(high, other, held), jnp.where(high, held, other)], 0
-        )
-    return held.astype(F32)
+            [jnp.where(high, other, held), jnp.where(high, held, other)], 1
+        )
+    return (held.astype(F32), *done, *(make(x) for make, x in work))
 
 
 def on_device(field_in, filter_weight, filter_basis, halo_reach, grad_out):
@@ -196,13 +224,13 @@
     masked = masked_basis(filter_basis, halo_reach)
     masked_below = shifted(masked[count - 1 :], "lat", 1)
     masked_above = shifted(masked[:1], "lat", -1)
-    mixer = filter_weight.reshape(outs, kernels * chans)
+    mixer = filter_weight.transpose(1, 0, 2)
 
     factor = 1.0 / math.sqrt(lax.axis_size("lat") * count * out_width)
     total = count * out_width
     inner, weight_term = call(
         functools.partial(forward_kernel, kernels, halo, factor),
-        (sds((total, kernels * chans), BF16), sds((outs, kernels * chans), F32)),
+        (sds((total, kernels * chans), BF16), sds((kernels, outs, chans), F32)),
         [pltpu.VMEM((rows_own + 3, width + 2 * halo, chans), BF16)],
         10**10,
         own,
@@ -211,11 +239,6 @@
         forward_matrix(masked),
         grad_out.reshape(outs, total),
     )
-    grad_weight = summed(weight_term, "lat").reshape(outs, kernels, chans)
-
-    field_out = call(mix_kernel, sds((outs, total), BF16), [], 4 * 10**9, mixer, inner)
-    field_out = field_out.reshape(outs, count, out_width)
-
     pairs = backward_pairs(count, lat)
     blocks = -(-out_width // BACK_BLOCK)
     span = BACK_BLOCK + halo
@@ -226,17 +249,37 @@
         [all_grads[:, out_width - lead :], all_grads, all_grads[:, : length - lead - out_width]], 1
     )
     all_masked = jnp.concatenate([masked_below, masked, masked_above], 0)
-    back = call(
-        functools.partial(backward_kernel, kernels, pairs),
-        sds((rows_own, blocks * 2 * BACK_BLOCK, chans), BF16),
-        [pltpu.VMEM((count + 2, length, kernels * chans), BF16)],
-        14 * 10**9,
-        all_grads,
-        mixer,
-        backward_matrix(all_masked, pairs),
-    )
-    grad_in = back[:, :width].transpose(2, 0, 1)
-    return (field_out, grad_in, grad_weight)
+    back_mats = backward_matrix(all_masked, pairs)
+
+    def mix(given):
+        return call(
+            mix_kernel,
+            sds((total, outs), BF16),
+            [pltpu.VMEM((outs, kernels * chans), BF16)],
+            4 * 10**9,
+            mixer,
+            given,
+        )
+
+    def back(given):
+        return call(
+            functools.partial(backward_kernel, kernels, pairs),
+            sds((rows_own, width, chans), BF16),
+            [pltpu.VMEM((count + 2, length, kernels * chans), BF16)],
+            14 * 10**9,
+            given,
+            mixer,
+            back_mats,
+        )
+
+    grad_weight, grad_in, field_out = summed(
+        weight_term, "lat", [(back, all_grads), (mix, inner)]
+    )
+    return (
+        field_out.reshape(count, out_width, outs).transpose(2, 0, 1),
+        grad_in.transpose(2, 0, 1),
+        grad_weight.transpose(1, 0, 2),
+    )
 
 
 def solution(mesh):

time: 209 us -> 182 us (0.87)
  local copies, waits for them, and re-layouts: 45.6 us -> 22.1 us
  other arithmetic: 14.3 us -> 10.2 us
    ppermute x4, waiting for transfers between devices: 28.3 us -> 8.13 us  [the longest x2 8.12 us: summed(): other = lax.ppermute(sent, axis, pairs)]
    ppermute x4, waiting for transfers between devices: 16.3 us -> 35.6 us  [summed(): other = lax.ppermute(held, axis, pairs)]
    unnamed x31 -> x21, local copies, waits for them, and re-layouts: 11.4 us -> 0.39 us
    reshape x1 -> x0, local copies, waits for them, and re-layouts: 4.34 us -> none  [on_device(): mixer = filter_weight.reshape(outs, kernels * chans)]
    convert_element_type x1 -> x0, other arithmetic: 4.08 us -> none  [summed(): return held.astype(F32)]
    transpose x1 -> x0, local copies, waits for them, and re-layouts: 3.62 us -> none  [on_device(): grad_in = back[:, :width].transpose(2, 0, 1)]
    ppermute x4, starting transfers between devices: 3.99 us -> 0.51 us  [summed(): other = lax.ppermute(held, axis, pairs)]
    ppermute x4, starting transfers between devices: 25.9 us -> 29 us  [the longest x2 24.5 us: summed(): other = lax.ppermute(sent, axis, pairs)]
  transfers between devices with their start and end apart: 14 -> 14, of which waited for: 5 -> 5; matrix products, arithmetic and copies ran while one was open for 19% -> 13% of each run, Pallas kernels for 16% -> 32%
where the time goes in v1:
time: 182 us; the launch traced here: 181 us
  Pallas kernels  58 us (32%)
  starting transfers between devices  45.5 us (25%)
  waiting for transfers between devices  43.7 us (24%)
  local copies, waits for them, and re-layouts  22.1 us (12%)
  other arithmetic  10.2 us (6%)
    pallas_call x3, Pallas kernels, call(): pl.pallas_call(body, out_shape=out_shape, in_specs=[whole] * len(args), o...  58 us
    ppermute x4, waiting for transfers between devices, summed(): other = lax.ppermute(held, axis, pairs)  35.6 us
    ppermute x2, starting transfers between devices, summed(): other = lax.ppermute(sent, axis, pairs)  24.5 us
    ppermute x6, starting transfers between devices, shifted(): return lax.ppermute(shard, axis, pairs)  16 us
    ppermute x2, waiting for transfers between devices, summed(): other = lax.ppermute(sent, axis, pairs)  8.12 us
    reshape x2, local copies, waits for them, and re-layouts, backward_matrix(): return spread.reshape(len(pairs) * 2 * BACK_BLOCK, kernels * span)  7.05 us
    ppermute x2, starting transfers between devices, summed(): other, made = tied(lax.ppermute(sent, axis, pairs), make(given))  4.57 us
  transfers between devices with their start and end apart: 14, of which 5 were waited for; matrix products, arithmetic and copies ran while one was open for 13% of the time, Pallas kernels for 32%

profile of v1, /device:TPU:0, one launch (start us, length us, event | category | flops | bytes accessed | tf_op | source)
XLA Modules:
  0.0 181.3 jit_solution(10252338935537118374)
XLA Ops:
  0.6 0.0 copy-start
  0.6 2.7 %slice.72 = bf16[2,1440,256]{2,1,0:T(8,128)(2,1)} slice(bf16[4,1440,256]{2,1,0:T(8,128)(2,1)} %bitcast.70), slice={[2:4], [0:1440], [0:256]} | slice | bytes 2949120 | tf_op jit(solution)/shard_map/slice | solution.py:219
  3.3 0.0 copy-start.4
  3.3 0.0 copy-start.1
  3.3 3.6 %collective-permute-start = (bf16[2,1440,256]{2,1,0:T(8,128)(2,1)}, bf16[2,1440,256]{2,1,0:T(8,128)(2,1)}, u32[]{:S(2)}, u32[]{:S(2)}) collective-permute-start(bf16[2,1440,256]{2,1,0:T(8,128)(2,1)} %slice.72), channel_id=1, source_target_pairs={{0,1},{1,2},{2,3},{3,4},{4,5},{5,6},{6,7},{7,8},{8,9},{9,10},{10,1... | collective-permute-start | bytes 4423688 | tf_op jit(solution)/shard_map/ppermute | solution.py:23
  7.0 2.0 %slice.73 = bf16[1,1440,256]{2,1,0:T(8,128)(2,1)} slice(bf16[4,1440,256]{2,1,0:T(8,128)(2,1)} %bitcast.71), slice={[0:1], [0:1440], [0:256]} | slice | bytes 1474560 | tf_op jit(solution)/shard_map/slice | solution.py:220
  9.0 1.3 collective-permute-start.1
  10.3 0.0 copy-done
  10.3 1.2 fusion.2
  11.5 1.3 collective-permute-start.4
  12.8 5.5 %collective-permute-start.3 = (bf16[1,720,512]{2,1,0:T(8,128)(2,1)}, bf16[1,720,512]{2,1,0:T(8,128)(2,1)}, u32[]{:S(2)}, u32[]{:S(2)}) collective-permute-start(bf16[1,720,512]{2,1,0:T(8,128)(2,1)} %get-tuple-element.25), channel_id=1, source_target_pairs={{0,1},{1,2},{2,3},{3,4},{4,5},{5,6},{6,7},{7,8},{8,9},{9,10},{10,1... | collective-permute-start | bytes 2211848 | tf_op jit(solution)/shard_map/ppermute | solution.py:23
  18.4 0.0 copy-done.4
  18.4 0.1 compare_convert_fusion
  18.4 0.0 copy-done.3
  18.5 2.8 %collective-permute-start.6 = (bf16[1,9,5,33]{3,1,2,0:T(8,128)(2,1)S(1)}, bf16[1,9,5,33]{3,1,2,0:T(8,128)(2,1)S(1)}, u32[]{:S(2)}, u32[]{:S(2)}) collective-permute-start(bf16[1,9,5,33]{3,1,2,0:T(8,128)(2,1)S(1)} %get-tuple-element.34), channel_id=1, source_target_pairs={{0,1},{1,2},{2,3},{3,4},{4,5},{5,6},{6,7},{7,8},{8,9},{9,10},{10,1... | collective-permute-start | bytes 8918 | tf_op jit(solution)/shard_map/ppermute | solution.py:23
  21.3 0.0 copy-done.1
  21.3 0.5 convolution_convert_fusion
  21.8 0.2 copy.30
  22.0 0.1 slice.88
  22.1 0.5 copy.33
  22.6 2.2 %reshape.61.mats = bf16[2,432,640]{2,1,0:T(8,128)(2,1)} reshape(bf16[2,9,48,5,128]{4,3,2,1,0:T(8,128)(2,1)S(1)} %bitcast.65) | data formatting | bytes 2211840 | tf_op jit(solution)/shard_map/reshape | solution.py:40
  24.8 1.6 copy.25.grad
  26.3 0.0 collective-permute-done.6
  26.3 1.5 collective-permute-start.7
  27.9 0.0 collective-permute-done.1.above
  27.9 0.0 collective-permute-done.below
  27.9 22.9 %shard_map.94 = (bf16[1440,2304]{1,0:T(8,128)(2,1)}, f32[9,512,256]{2,1,0:T(8,128)}) custom-call(bf16[4,1440,256]{2,1,0:T(8,128)(2,1)} %bitcast.72, bf16[2,1440,256]{2,1,0:T(8,128)(2,1)} %collective-permute-done.below, bf16[1,1440,256]{2,1,0:T(8,128)(2,1)} %collective-permute-done.1.above, bf16[2,432,640]{2,1,0:T(8,128)(2,1)} %reshape.61.mats, ...), custom_call_target="tpu_custom_call" | custom-call | flops 10000000000 | bytes 7741440 | tf_op jit(solution)/shard_map/pallas_call | solution.py:163
  50.9 2.8 %dynamic-slice_convert_fusion = bf16[9,256,256]{2,1,0:T(8,128)(2,1)} fusion(f32[9,512,256]{2,1,0:T(8,128)} %get-tuple-element.13, s32[]{:T(128)S(6)} %select_n.73), kind=kLoop, calls=%fused_computation.10 | loop fusion | bytes 2359300 | tf_op jit(solution)/shard_map/convert_element_type | solution.py:189
  53.7 23.4 %collective-permute-start.2 = (bf16[9,256,256]{2,1,0:T(8,128)(2,1)}, bf16[9,256,256]{2,1,0:T(8,128)(2,1)}, u32[]{:S(2)}, u32[]{:S(2)}) collective-permute-start(bf16[9,256,256]{2,1,0:T(8,128)(2,1)} %dynamic-slice_convert_fusion), channel_id=1, source_target_pairs={{0,1},{1,0},{2,3},{3,2},{4,5},{5,4},{6,7},{7,6},{8,9},{9,8},{10,11... | collective-permute-start | bytes 3538952 | tf_op jit(solution)/shard_map/ppermute | solution.py:197
  77.1 0.0 collective-permute-done.7
  77.1 0.0 copy-done.2
  77.2 0.3 convolution_convert_fusion.1
  77.5 1.5 reshape.64
  79.0 2.8 %copy.28 = bf16[10,64,9,48]{3,2,1,0:T(8,128)(2,1)} copy(bf16[10,64,9,48]{3,1,2,0:T(8,128)(2,1)S(1)} %bitcast.66) | data formatting | bytes 1105920 | tf_op jit(solution)/shard_map/reshape | solution.py:61
  81.7 4.3 %reshape.67.mats = bf16[640,432]{1,0:T(8,128)(2,1)} reshape(bf16[10,64,9,48]{3,2,1,0:T(8,128)(2,1)} %copy.28) | data formatting | bytes 1105920 | tf_op jit(solution)/shard_map/reshape | solution.py:61
  86.0 0.0 collective-permute-done.4
  86.0 0.0 collective-permute-done.3
  86.0 2.9 %fusion.grads = bf16[4,752,512]{2,1,0:T(8,128)(2,1)} fusion(bf16[1,720,512]{2,1,0:T(8,128)(2,1)} %collective-permute-done.4, bf16[2,720,512]{2,1,0:T(8,128)(2,1)S(1)} %bitcast.64, bf16[1,720,512]{2,1,0:T(8,128)(2,1)} %collective-permute-done.3), kind=kLoop, calls=%fused_computation.4 | loop fusion | flops 27721728 | bytes 6029312 | tf_op jit(solution)/shard_map/concatenate | solution.py:248
  88.9 0.0 collective-permute-done.2
  88.9 2.3 %convert_add_fusion = f32[9,256,256]{2,1,0:T(8,128)S(1)} fusion(bf16[9,256,256]{2,1,0:T(8,128)(2,1)} %collective-permute-done.2, f32[9,512,256]{2,1,0:T(8,128)} %get-tuple-element.13, s32[]{:T(128)S(6)} %select_n.72), kind=kLoop, calls=%fused_computation.9 | loop fusion | flops 1179648 | bytes 5898244 | tf_op jit(solution)/shard_map/add | solution.py:198
  91.2 0.1 dynamic-slice_convert_fusion.1
  91.3 2.9 %collective-permute-start.5 = (bf16[9,128,256]{2,1,0:T(8,128)(2,1)S(1)}, bf16[9,128,256]{2,1,0:T(8,128)(2,1)S(1)}, u32[]{:S(2)}, u32[]{:S(2)}) collective-permute-start(bf16[9,128,256]{2,1,0:T(8,128)(2,1)S(1)} %dynamic-slice_convert_fusion.1), channel_id=1, source_target_pairs={{0,2},{1,3},{2,0},{3,1},{4,6},{5,7},{6,4},{7,5},{8,10},{9,11},{10,... | collective-permute-start | bytes 1769480 | tf_op jit(solution)/shard_map/ppermute | solution.py:194
  94.2 25.3 %shard_map.95 = bf16[4,1440,256]{2,1,0:T(8,128)(2,1)} custom-call(bf16[4,752,512]{2,1,0:T(8,128)(2,1)} %fusion.grads, bf16[9,512,256]{2,1,0:T(8,128)(2,1)} %bitcast.73, bf16[640,432]{1,0:T(8,128)(2,1)} %reshape.67.mats), custom_call_target="tpu_custom_call" | custom-call | flops 14000000000 | bytes 5992448 | tf_op jit(solution)/shard_map/pallas_call | solution.py:163
  119.6 0.0 collective-permute-done.5
  119.6 0.1 convert_add_fusion.1
  119.8 1.6 collective-permute-start.8
  121.4 9.7 %shard_map.96 = bf16[1440,512]{1,0:T(8,128)(2,1)} custom-call(bf16[9,512,256]{2,1,0:T(8,128)(2,1)} %bitcast.74, bf16[1440,2304]{1,0:T(8,128)(2,1)} %get-tuple-element.19.inner), custom_call_target="tpu_custom_call" | custom-call | flops 4000000000 | bytes 8994816 | tf_op jit(solution)/shard_map/pallas_call | solution.py:163
  131.1 0.0 collective-permute-done.8
  131.1 0.1 convert_add_fusion.2
  131.2 1.1 collective-permute-start.9
  132.3 8.1 %collective-permute-done.9 = bf16[9,32,256]{2,1,0:T(8,128)(2,1)S(1)} collective-permute-done((bf16[9,32,256]{2,1,0:T(8,128)(2,1)S(1)}, bf16[9,32,256]{2,1,0:T(8,128)(2,1)S(1)}, u32[]{:S(2)}, u32[]{:S(2)}) %collective-permute-start.9) | collective-permute-done | bytes 147488 | tf_op jit(solution)/shard_map/ppermute | solution.py:197
  140.5 0.1 collective-permute-start.10
  140.6 9.5 %collective-permute-done.10 = bf16[9,32,256]{2,1,0:T(8,128)(2,1)S(1)} collective-permute-done((bf16[9,32,256]{2,1,0:T(8,128)(2,1)S(1)}, bf16[9,32,256]{2,1,0:T(8,128)(2,1)S(1)}, u32[]{:S(2)}, u32[]{:S(2)}) %collective-permute-start.10) | collective-permute-done | bytes 147488 | tf_op jit(solution)/shard_map/ppermute | solution.py:203
  150.1 0.1 collective-permute-start.11
  150.2 8.9 %collective-permute-done.11 = bf16[9,64,256]{2,1,0:T(8,128)(2,1)S(1)} collective-permute-done((bf16[9,64,256]{2,1,0:T(8,128)(2,1)S(1)}, bf16[9,64,256]{2,1,0:T(8,128)(2,1)S(1)}, u32[]{:S(2)}, u32[]{:S(2)}) %collective-permute-start.11) | collective-permute-done | bytes 294944 | tf_op jit(solution)/shard_map/ppermute | solution.py:203
  159.1 0.1 broadcast_select_fusion.5
  159.3 0.4 collective-permute-start.12
  159.6 14.1 %collective-permute-done.12 = bf16[9,128,256]{2,1,0:T(8,128)(2,1)S(1)} collective-permute-done((bf16[9,128,256]{2,1,0:T(8,128)(2,1)S(1)}, bf16[9,128,256]{2,1,0:T(8,128)(2,1)S(1)}, u32[]{:S(2)}, u32[]{:S(2)}) %collective-permute-start.12) | collective-permute-done | bytes 589856 | tf_op jit(solution)/shard_map/ppermute | solution.py:203
  173.8 0.2 broadcast_select_fusion.3
  174.0 1.1 pad_maximum_fusion.4
  175.1 0.0 collective-permute-start.13
  175.1 3.1 %collective-permute-done.13 = bf16[9,256,256]{2,1,0:T(8,128)(2,1)S(1)} collective-permute-done((bf16[9,256,256]{2,1,0:T(8,128)(2,1)}, bf16[9,256,256]{2,1,0:T(8,128)(2,1)S(1)}, u32[]{:S(2)}, u32[]{:S(2)}) %collective-permute-start.13) | collective-permute-done | bytes 1179680 | tf_op jit(solution)/shard_map/ppermute | solution.py:203
  178.2 0.5 broadcast_select_fusion.1
  178.6 2.6 %convert_bitcast_fusion = f32[512,9,256]{2,0,1:T(8,128)} fusion(bf16[9,256,256]{2,1,0:T(8,128)(2,1)S(1)} %get-tuple-element.24, bf16[9,256,256]{2,1,0:T(8,128)(2,1)S(1)} %get-tuple-element.23), kind=kLoop, calls=%fused_computation.1 | loop fusion | flops 4718592 | bytes 7077888 | tf_op jit(solution)/shard_map/transpose | solution.py:281
  (24 shorter events, 0.4 us)
Async XLA Ops:
  0.6 9.7 %copy-start = (bf16[512,2,720]{0,2,1:T(8,128)(2,1)S(1)}, bf16[512,2,720]{0,2,1:T(8,128)(2,1)}, u32[]{:S(2)}) copy-start(bf16[512,2,720]{0,2,1:T(8,128)(2,1)} %param.11) | copy-start | bytes 4423684
  3.3 15.0 %copy-start.4 = (s32[2]{0:T(128)S(1)}, s32[2]{0:T(128)}, u32[]{:S(2)}) copy-start(s32[2]{0:T(128)} %param.10) | copy-start | bytes 28
  3.3 15.1 %copy-start.3 = (bf16[2,9,5,33]{3,0,2,1:T(2,128)(2,1)S(1)}, bf16[2,9,5,33]{3,0,2,1:T(2,128)(2,1)}, u32[]{:S(2)}) copy-start(bf16[2,9,5,33]{3,0,2,1:T(2,128)(2,1)} %param.9) | copy-start | bytes 17824
  3.3 18.0 %copy-start.1 = (bf16[33,6144]{1,0:T(8,128)(2,1)S(1)}, bf16[33,6144]{1,0:T(8,128)(2,1)}, u32[]{:S(2)}) copy-start(bf16[33,6144]{1,0:T(8,128)(2,1)} %constant.29.clone) | copy-start | bytes 1216516
  3.3 24.6 %collective-permute-start = (bf16[2,1440,256]{2,1,0:T(8,128)(2,1)}, bf16[2,1440,256]{2,1,0:T(8,128)(2,1)}, u32[]{:S(2)}, u32[]{:S(2)}) collective-permute-start(bf16[2,1440,256]{2,1,0:T(8,128)(2,1)} %slice.72), channel_id=1, source_target_pairs={{0,1},{1,2},{2,3},{3,4},{4,5},{5,6},{6,7},{7,8},{8,9},{9,10},{10,1... | collective-permute-start | bytes 4423688 | tf_op jit(solution)/shard_map/ppermute | solution.py:23
  9.0 18.9 %collective-permute-start.1 = (bf16[1,1440,256]{2,1,0:T(8,128)(2,1)}, bf16[1,1440,256]{2,1,0:T(8,128)(2,1)}, u32[]{:S(2)}, u32[]{:S(2)}) collective-permute-start(bf16[1,1440,256]{2,1,0:T(8,128)(2,1)} %slice.73), channel_id=1, source_target_pairs={{1,0},{2,1},{3,2},{4,3},{5,4},{6,5},{7,6},{8,7},{9,8},{10,9},{11,1... | collective-permute-start | bytes 2211848 | tf_op jit(solution)/shard_map/ppermute | solution.py:23
  11.5 74.5 %collective-permute-start.4 = (bf16[1,720,512]{2,1,0:T(8,128)(2,1)}, bf16[1,720,512]{2,1,0:T(8,128)(2,1)}, u32[]{:S(2)}, u32[]{:S(2)}) collective-permute-start(bf16[1,720,512]{2,1,0:T(8,128)(2,1)} %get-tuple-element.26), channel_id=1, source_target_pairs={{1,0},{2,1},{3,2},{4,3},{5,4},{6,5},{7,6},{8,7},{9,8},{10,9},{11,1... | collective-permute-start | bytes 2211848 | tf_op jit(solution)/shard_map/ppermute | solution.py:23
  12.8 73.2 %collective-permute-start.3 = (bf16[1,720,512]{2,1,0:T(8,128)(2,1)}, bf16[1,720,512]{2,1,0:T(8,128)(2,1)}, u32[]{:S(2)}, u32[]{:S(2)}) collective-permute-start(bf16[1,720,512]{2,1,0:T(8,128)(2,1)} %get-tuple-element.25), channel_id=1, source_target_pairs={{0,1},{1,2},{2,3},{3,4},{4,5},{5,6},{6,7},{7,8},{8,9},{9,10},{10,1... | collective-permute-start | bytes 2211848 | tf_op jit(solution)/shard_map/ppermute | solution.py:23
  18.5 7.9 %collective-permute-start.6 = (bf16[1,9,5,33]{3,1,2,0:T(8,128)(2,1)S(1)}, bf16[1,9,5,33]{3,1,2,0:T(8,128)(2,1)S(1)}, u32[]{:S(2)}, u32[]{:S(2)}) collective-permute-start(bf16[1,9,5,33]{3,1,2,0:T(8,128)(2,1)S(1)} %get-tuple-element.34), channel_id=1, source_target_pairs={{0,1},{1,2},{2,3},{3,4},{4,5},{5,6},{6,7},{7,8},{8,9},{9,10},{10,1... | collective-permute-start | bytes 8918 | tf_op jit(solution)/shard_map/ppermute | solution.py:23
  26.3 50.8 %collective-permute-start.7 = (bf16[1,9,5,33]{3,1,2,0:T(8,128)(2,1)S(1)}, bf16[1,9,5,33]{3,1,2,0:T(8,128)(2,1)S(1)}, u32[]{:S(2)}, u32[]{:S(2)}) collective-permute-start(bf16[1,9,5,33]{3,1,2,0:T(8,128)(2,1)S(1)} %get-tuple-element.33), channel_id=1, source_target_pairs={{1,0},{2,1},{3,2},{4,3},{5,4},{6,5},{7,6},{8,7},{9,8},{10,9},{11,1... | collective-permute-start | bytes 8918 | tf_op jit(solution)/shard_map/ppermute | solution.py:23
  50.9 26.3 %copy-start.2 = (bf16[33,3072]{1,0:T(8,128)(2,1)S(1)}, bf16[33,3072]{1,0:T(8,128)(2,1)}, u32[]{:S(2)}) copy-start(bf16[33,3072]{1,0:T(8,128)(2,1)} %constant.30.clone) | copy-start | bytes 608260
  53.7 35.2 %collective-permute-start.2 = (bf16[9,256,256]{2,1,0:T(8,128)(2,1)}, bf16[9,256,256]{2,1,0:T(8,128)(2,1)}, u32[]{:S(2)}, u32[]{:S(2)}) collective-permute-start(bf16[9,256,256]{2,1,0:T(8,128)(2,1)} %dynamic-slice_convert_fusion), channel_id=1, source_target_pairs={{0,1},{1,0},{2,3},{3,2},{4,5},{5,4},{6,7},{7,6},{8,9},{9,8},{10,11... | collective-permute-start | bytes 3538952 | tf_op jit(solution)/shard_map/ppermute | solution.py:197
  91.3 28.3 %collective-permute-start.5 = (bf16[9,128,256]{2,1,0:T(8,128)(2,1)S(1)}, bf16[9,128,256]{2,1,0:T(8,128)(2,1)S(1)}, u32[]{:S(2)}, u32[]{:S(2)}) collective-permute-start(bf16[9,128,256]{2,1,0:T(8,128)(2,1)S(1)} %dynamic-slice_convert_fusion.1), channel_id=1, source_target_pairs={{0,2},{1,3},{2,0},{3,1},{4,6},{5,7},{6,4},{7,5},{8,10},{9,11},{10,... | collective-permute-start | bytes 1769480 | tf_op jit(solution)/shard_map/ppermute | solution.py:194
  119.8 11.3 %collective-permute-start.8 = (bf16[9,64,256]{2,1,0:T(8,128)(2,1)S(1)}, bf16[9,64,256]{2,1,0:T(8,128)(2,1)S(1)}, u32[]{:S(2)}, u32[]{:S(2)}) collective-permute-start(bf16[9,64,256]{2,1,0:T(8,128)(2,1)S(1)} %dynamic-slice_convert_fusion.2), channel_id=1, source_target_pairs={{0,4},{1,5},{2,6},{3,7},{4,0},{5,1},{6,2},{7,3},{8,12},{9,13},{10,... | collective-permute-start | bytes 884744 | tf_op jit(solution)/shard_map/ppermute | solution.py:194
  131.2 9.2 %collective-permute-start.9 = (bf16[9,32,256]{2,1,0:T(8,128)(2,1)S(1)}, bf16[9,32,256]{2,1,0:T(8,128)(2,1)S(1)}, u32[]{:S(2)}, u32[]{:S(2)}) collective-permute-start(bf16[9,32,256]{2,1,0:T(8,128)(2,1)S(1)} %dynamic-slice_convert_fusion.3), channel_id=1, source_target_pairs={{0,8},{1,9},{2,10},{3,11},{4,12},{5,13},{6,14},{7,15},{8,0},{9,1},... | collective-permute-start | bytes 442376 | tf_op jit(solution)/shard_map/ppermute | solution.py:197
  140.5 9.6 %collective-permute-start.10 = (bf16[9,32,256]{2,1,0:T(8,128)(2,1)S(1)}, bf16[9,32,256]{2,1,0:T(8,128)(2,1)S(1)}, u32[]{:S(2)}, u32[]{:S(2)}) collective-permute-start(bf16[9,32,256]{2,1,0:T(8,128)(2,1)S(1)} %add_convert_fusion), channel_id=1, source_target_pairs={{0,8},{1,9},{2,10},{3,11},{4,12},{5,13},{6,14},{7,15},{8,0},{9,1},... | collective-permute-start | bytes 442376 | tf_op jit(solution)/shard_map/ppermute | solution.py:203
  150.1 9.0 %collective-permute-start.11 = (bf16[9,64,256]{2,1,0:T(8,128)(2,1)S(1)}, bf16[9,64,256]{2,1,0:T(8,128)(2,1)S(1)}, u32[]{:S(2)}, u32[]{:S(2)}) collective-permute-start(bf16[9,64,256]{2,1,0:T(8,128)(2,1)S(1)} %pad_maximum_fusion.6), channel_id=1, source_target_pairs={{0,4},{1,5},{2,6},{3,7},{4,0},{5,1},{6,2},{7,3},{8,12},{9,13},{10,... | collective-permute-start | bytes 884744 | tf_op jit(solution)/shard_map/ppermute | solution.py:203
  159.3 14.5 %collective-permute-start.12 = (bf16[9,128,256]{2,1,0:T(8,128)(2,1)S(1)}, bf16[9,128,256]{2,1,0:T(8,128)(2,1)S(1)}, u32[]{:S(2)}, u32[]{:S(2)}) collective-permute-start(bf16[9,128,256]{2,1,0:T(8,128)(2,1)S(1)} %pad_maximum_fusion.5), channel_id=1, source_target_pairs={{0,2},{1,3},{2,0},{3,1},{4,6},{5,7},{6,4},{7,5},{8,10},{9,11},{10,... | collective-permute-start | bytes 1769480 | tf_op jit(solution)/shard_map/ppermute | solution.py:203
  175.1 3.1 %collective-permute-start.13 = (bf16[9,256,256]{2,1,0:T(8,128)(2,1)}, bf16[9,256,256]{2,1,0:T(8,128)(2,1)S(1)}, u32[]{:S(2)}, u32[]{:S(2)}) collective-permute-start(bf16[9,256,256]{2,1,0:T(8,128)(2,1)} %pad_maximum_fusion.4), channel_id=1, source_target_pairs={{0,1},{1,0},{2,3},{3,2},{4,5},{5,4},{6,7},{7,6},{8,9},{9,8},{10,11... | collective-permute-start | bytes 3538952 | tf_op jit(solution)/shard_map/ppermute | solution.py:203

commit v2 on v1

--- a/solution.py
+++ b/solution.py
@@ -96,40 +96,118 @@
     lax.fori_loop(0, kernels, column, 0)
 
 
-def mix_kernel(mixer, inner, out, wide):
+def exchange_kernel(
+    kernels, pairs, size, term, inner, mixer, grads, mats,
+    weight, field, back, held, wide, acc, sent, got, send_sem, recv_sem,
+):
+    steps = size.bit_length() - 1
+    outs, chans = term.shape[1:]
+    me = lax.axis_index("lat")
+    bits = [lax.rem(me // (1 << s), 2) for s in range(steps)]
+    partners = [me + (1 - 2 * bits[s]) * (1 << s) for s in range(steps)]
+    halves = [outs >> (s + 1) for s in range(steps)]
+    barrier = pltpu.get_barrier_semaphore()
+    for partner in partners:
+        pl.semaphore_signal(
+            barrier, inc=1, device_id={"lat": partner}, device_id_type=pl.DeviceIdType.MESH
+        )
+    pl.semaphore_wait(barrier, steps)
+
+    cut = (kernels + 1) // 2
+    chunks = [slice(0, cut), slice(cut, kernels)]
+
+    def place(first, s):
+        return sum((bits[t] * halves[t] for t in range(first, s)), 0 * me)
+
+    def rows(start, count):
+        return pl.ds(pl.multiple_of(start, 16), count)
+
+    def copy(c, t, source, target, s):
+        made = pltpu.make_async_remote_copy(
+            src_ref=source,
+            dst_ref=target,
+            send_sem=send_sem.at[c, t],
+            recv_sem=recv_sem.at[c, t],
+            device_id={"lat": partners[s]},
+            device_id_type=pl.DeviceIdType.MESH,
+        )
+        made.start()
+        return made
+
+    def start(c, t):
+        ks = chunks[c]
+        if t < steps:
+            h, lag = halves[t], outs - (outs >> t)
+            source = term if t == 0 else acc
+            away = rows(place(1, t) + (1 - bits[t]) * h, h)
+            sent[ks, lag : lag + h] = source[ks, away].astype(BF16)
+            return copy(c, t, sent.at[ks, lag : lag + h], got.at[ks, lag : lag + h], t)
+        s = 2 * steps - 1 - t
+        if t == steps:
+            last = halves[-1]
+            weight[ks, rows(place(0, steps), last)] = acc[ks, rows(place(1, steps), last)].astype(BF16)
+        mine = weight.at[ks, rows(place(0, s + 1), halves[s])]
+        return copy(c, t, mine, mine, s)
+
+    def finish(c, t, made):
+        ks = chunks[c]
+        made.wait()
+        if t < steps:
+            h, lag = halves[t], outs - (outs >> t)
+            arrived = got[ks, lag : lag + h].astype(F32)
+            at = rows(place(1, t) + bits[t] * h, h)
+            if t == 0:
+                acc[ks] = term[ks, at] + arrived
+            else:
+                acc[ks, at] = acc[ks, at] + arrived
+
+    units = back_units(kernels, pairs, grads, mixer, mats, back, held)
+    units[4:4] = mix_units(mixer, inner, field, wide)
+    flying = [start(c, 0) for c in range(2)]
+    slots, done = 4 * steps, 0
+    for t in range(2 * steps):
+        for c in range(2):
+            until = -(-len(units) * (2 * t + c + 1) // slots)
+            for unit in units[done:until]:
+                unit()
+            done = until
+            finish(c, t, flying[c])
+            if t + 1 < 2 * steps:
+                flying[c] = start(c, t + 1)
+
+
+def mix_units(mixer, inner, out, wide):
     kernels, _, chans = mixer.shape
-    for k in range(kernels):
-        wide[:, k * chans : (k + 1) * chans] = mixer[k]
-    total = inner.shape[0]
-    rows = total // MIX_PARTS
-
-    def part(n, carry):
-        at = pl.ds(pl.multiple_of(n * rows, 16), rows)
+    rows = inner.shape[0] // MIX_PARTS
+
+    def spread():
+        for k in range(kernels):
+            wide[:, k * chans : (k + 1) * chans] = mixer[k]
+
+    def part(n):
+        at = slice(n * rows, (n + 1) * rows)
         got = lax.dot_general(
             inner[at], wide[...], (((1,), (1,)), ((), ())), preferred_element_type=F32
         )
         out[at] = got.astype(BF16)
-        return carry
-
-    lax.fori_loop(0, MIX_PARTS, part, 0)
-
-
-def backward_kernel(kernels, pairs, grads, mixer, mats, out, held):
-    nrows, length, _ = grads.shape
+
+    return [spread] + [functools.partial(part, n) for n in range(MIX_PARTS)]
+
+
+def back_units(kernels, pairs, grads, mixer, mats, out, held):
+    nrows = grads.shape[0]
     chans = mixer.shape[2]
     span = mats.shape[1] // kernels
     step = 2 * BACK_BLOCK
-    for i in range(nrows):
-
-        def column(k, carry, i=i):
+    width = out.shape[1]
+
+    def columns(i, first, last):
+        def column(k, carry):
             at = pl.ds(pl.multiple_of(k * chans, chans), chans)
-            got = jnp.dot(grads[i], mixer[k], preferred_element_type=F32)
-            held[i, :, at] = got.astype(BF16)
+            held[i, :, at] = jnp.dot(grads[i], mixer[k], preferred_element_type=F32).astype(BF16)
             return carry
 
-        lax.fori_loop(0, kernels, column, 0)
-
-    width = out.shape[1]
+        lax.fori_loop(first, last, column, 0)
 
     def block(b, size):
         start = pl.multiple_of(b * BACK_BLOCK, 16)
@@ -148,16 +226,27 @@
         for q, value in enumerate(sums):
             out[q, pl.ds(pl.multiple_of(b * step, 32), size), :] = value[:size].astype(BF16)
 
-    def whole_block(b, carry):
-        block(b, step)
-        return carry
-
-    lax.fori_loop(0, width // step, whole_block, 0)
+    def blocks(first, last):
+        def whole_block(b, carry):
+            block(b, step)
+            return carry
+
+        lax.fori_loop(first, last, whole_block, 0)
+
+    cut = (kernels + 1) // 2
+    units = []
+    for i in range(nrows):
+        units.append(functools.partial(columns, i, 0, cut))
+        units.append(functools.partial(columns, i, cut, kernels))
+    full = width // step
+    for first in range(0, full, 4):
+        units.append(functools.partial(blocks, first, min(first + 4, full)))
     if width % step:
-        block(width // step, width % step)
-
-
-def call(body, out_shape, scratch, flops, *args):
+        units.append(functools.partial(block, full, width % step))
+    return units
+
+
+def call(body, out_shape, scratch, flops, *args, **params):
     n_bytes = sum(a.size * a.dtype.itemsize for a in args)
     whole = pl.BlockSpec(memory_space=pltpu.VMEM)
     return pl.pallas_call(
@@ -166,45 +255,9 @@
         in_specs=[whole] * len(args),
         out_specs=jax.tree.map(lambda _: whole, out_shape),
         scratch_shapes=scratch,
-        compiler_params=pltpu.CompilerParams(vmem_limit_bytes=VMEM_LIMIT),
+        compiler_params=pltpu.CompilerParams(vmem_limit_bytes=VMEM_LIMIT, **params),
         cost_estimate=pl.CostEstimate(flops=flops, bytes_accessed=n_bytes, transcendentals=0),
     )(*args)
-
-
-def tied(value, *others):
-    return lax.optimization_barrier((value, *others))
-
-
-def summed(term, axis, work):
-    size = lax.axis_size(axis)
-    steps = size.bit_length() - 1
-    if size != 1 << steps or term.shape[1] % size:
-        return (lax.psum(term, axis), *(make(x) for make, x in work))
-    me = lax.axis_index(axis)
-    done = []
-    for bit in range(steps):
-        half = term.shape[1] // 2
-        pairs = [(i, i ^ (1 << bit)) for i in range(size)]
-        high = (me >> bit) & 1
-        sent = lax.dynamic_slice_in_dim(term, (1 - high) * half, half, 1).astype(BF16)
-        kept = lax.dynamic_slice_in_dim(term, high * half, half, 1)
-        if bit > 0 and work:
-            (make, given), work = work[0], work[1:]
-            sent, given = tied(sent, given)
-            other, made = tied(lax.ppermute(sent, axis, pairs), make(given))
-            done.append(made)
-        else:
-            other = lax.ppermute(sent, axis, pairs)
-        term = kept + other.astype(F32)
-    held = term.astype(BF16)
-    for bit in reversed(range(steps)):
-        pairs = [(i, i ^ (1 << bit)) for i in range(size)]
-        high = ((me >> bit) & 1) == 1
-        other = lax.ppermute(held, axis, pairs)
-        held = jnp.concatenate(
-            [jnp.where(high, other, held), jnp.where(high, held, other)], 1
-        )
-    return (held.astype(F32), *done, *(make(x) for make, x in work))
 
 
 def on_device(field_in, filter_weight, filter_basis, halo_reach, grad_out):
@@ -251,30 +304,35 @@
     all_masked = jnp.concatenate([masked_below, masked, masked_above], 0)
     back_mats = backward_matrix(all_masked, pairs)
 
-    def mix(given):
-        return call(
-            mix_kernel,
+    size = lax.axis_size("lat")
+    steps = size.bit_length() - 1
+    moved = outs - outs // size
+    grad_weight, field_out, grad_in = call(
+        functools.partial(exchange_kernel, kernels, pairs, size),
+        (
+            sds((kernels, outs, chans), BF16),
             sds((total, outs), BF16),
-            [pltpu.VMEM((outs, kernels * chans), BF16)],
-            4 * 10**9,
-            mixer,
-            given,
-        )
-
-    def back(given):
-        return call(
-            functools.partial(backward_kernel, kernels, pairs),
             sds((rows_own, width, chans), BF16),
-            [pltpu.VMEM((count + 2, length, kernels * chans), BF16)],
-            14 * 10**9,
-            given,
-            mixer,
-            back_mats,
-        )
-
-    grad_weight, grad_in, field_out = summed(
-        weight_term, "lat", [(back, all_grads), (mix, inner)]
-    )
+        ),
+        [
+            pltpu.VMEM((count + 2, length, kernels * chans), BF16),
+            pltpu.VMEM((outs, kernels * chans), BF16),
+            pltpu.VMEM((kernels, outs // 2, chans), F32),
+            pltpu.VMEM((kernels, moved, chans), BF16),
+            pltpu.VMEM((kernels, moved, chans), BF16),
+            pltpu.SemaphoreType.DMA((2, 2 * steps)),
+            pltpu.SemaphoreType.DMA((2, 2 * steps)),
+        ],
+        18 * 10**9,
+        weight_term,
+        inner,
+        mixer,
+        all_grads,
+        back_mats,
+        collective_id=0,
+        has_side_effects=True,
+    )
+    grad_weight = grad_weight.astype(F32)
     return (
         field_out.reshape(count, out_width, outs).transpose(2, 0, 1),
         grad_in.transpose(2, 0, 1),

time: 182 us -> 154 us (0.85)
  waiting for transfers between devices: 43.7 us -> 0.02 us
  Pallas kernels: 58 us -> 101 us
  starting transfers between devices: 45.5 us -> 17.4 us
  matrix products: 0.76 us -> 2.75 us
    ppermute x8 -> x0, waiting for transfers between devices: 43.7 us -> none  [the longest x4 35.6 us: summed(): other = lax.ppermute(held, axis, pairs)]
    pallas_call x3 -> x2, Pallas kernels: 58 us -> 101 us  [call(): pl.pallas_call(body, out_shape=out_shape, in_specs=[whole] * len(args), o...]
    ppermute x8 -> x0, starting transfers between devices: 29.6 us -> none  [the longest x2 24.5 us: summed(): other = lax.ppermute(sent, axis, pairs)]
    unnamed x21, local copies, waits for them, and re-layouts: 0.39 us -> 4.34 us
    convert_element_type x4 -> x0, local copies, waits for them, and re-layouts: 2.98 us -> none  [summed(): lax.dynamic_slice_in_dim(term, (1 - high) * half, half, 1).astype(BF16)]
    add x3 -> x0, other arithmetic: 2.51 us -> none  [summed(): term = kept + other.astype(F32)]
  transfers between devices with their start and end apart: 14 -> 6, of which waited for: 5 -> 0; matrix products, arithmetic and copies ran while one was open for 13% -> 16% of each run, Pallas kernels for 32% -> 0%
where the time goes in v2:
time: 154 us
  Pallas kernels  101 us (66%)
  local copies, waits for them, and re-layouts  23.1 us (15%)
  starting transfers between devices  17.4 us (11%)
  other arithmetic  8.82 us (6%)
  matrix products  2.75 us (2%)
    pallas_call x2, Pallas kernels, call(): pl.pallas_call(body, out_shape=out_shape, in_specs=[whole] * len(args), o...  101 us
    ppermute x6, starting transfers between devices, shifted(): return lax.ppermute(shard, axis, pairs)  17.4 us
    reshape x2, local copies, waits for them, and re-layouts, backward_matrix(): return spread.reshape(len(pairs) * 2 * BACK_BLOCK, kernels * span)  7.05 us
    transpose x1, other arithmetic, on_device(): grad_weight.transpose(1, 0, 2)  4.41 us
    unnamed x21, local copies, waits for them, and re-layouts  4.34 us
  transfers between devices with their start and end apart: 6, of which 0 were waited for; matrix products, arithmetic and copies ran while one was open for 16% of the time, Pallas kernels for 0%

profile of v2, /device:TPU:0, one launch (start us, length us, event | category | flops | bytes accessed | tf_op | source)
XLA Modules:
  0.0 154.0 jit_solution(12754024623866007688)
XLA Ops:
  0.6 0.7 compare_convert_fusion
  1.4 0.7 copy_multiply_fusion
  2.1 1.3 collective-permute-start.5
  3.4 3.0 %collective-permute-start.4 = (bf16[1,9,5,33]{3,1,2,0:T(8,128)(2,1)S(1)}, bf16[1,9,5,33]{3,1,2,0:T(8,128)(2,1)S(1)}, u32[]{:S(2)}, u32[]{:S(2)}) collective-permute-start(bf16[1,9,5,33]{3,1,2,0:T(8,128)(2,1)S(1)} %get-tuple-element.16), channel_id=1, source_target_pairs={{0,1},{1,2},{2,3},{3,4},{4,5},{5,6},{6,7},{7,8},{8,9},{9,10},{10,1... | collective-permute-start | bytes 8918 | tf_op jit(solution)/shard_map/ppermute | solution.py:23
  6.5 0.0 copy-start.2
  6.5 2.2 %slice.73 = bf16[1,1440,256]{2,1,0:T(8,128)(2,1)} slice(bf16[4,1440,256]{2,1,0:T(8,128)(2,1)} %bitcast.71), slice={[0:1], [0:1440], [0:256]} | slice | bytes 1474560 | tf_op jit(solution)/shard_map/slice | solution.py:273
  8.7 1.3 collective-permute-start.1
  9.9 2.6 %fusion.2 = (bf16[1,720,512]{2,1,0:T(8,128)(2,1)}, bf16[1,720,512]{2,1,0:T(8,128)(2,1)}) fusion(bf16[2,720,512]{2,1,0:T(8,128)(2,1)} %bitcast.62), kind=kLoop, calls=%fused_computation.33 | loop fusion | bytes 2949120 | tf_op jit(solution)/shard_map/slice | solution.py:275
  12.5 6.0 %collective-permute-start.2 = (bf16[1,720,512]{2,1,0:T(8,128)(2,1)}, bf16[1,720,512]{2,1,0:T(8,128)(2,1)}, u32[]{:S(2)}, u32[]{:S(2)}) collective-permute-start(bf16[1,720,512]{2,1,0:T(8,128)(2,1)} %get-tuple-element.13), channel_id=1, source_target_pairs={{0,1},{1,2},{2,3},{3,4},{4,5},{5,6},{6,7},{7,8},{8,9},{9,10},{10,1... | collective-permute-start | bytes 2211848 | tf_op jit(solution)/shard_map/ppermute | solution.py:23
  18.5 1.3 collective-permute-start.3
  19.8 1.5 convolution_convert_fusion
  21.4 0.0 copy-done.2
  21.4 1.2 slice.72
  22.6 0.2 copy.30
  22.8 0.1 slice.88
  22.9 0.0 copy-start
  22.9 0.5 copy.33
  23.4 2.1 %reshape.61.mats = bf16[2,432,640]{2,1,0:T(8,128)(2,1)} reshape(bf16[2,9,48,5,128]{4,3,2,1,0:T(8,128)(2,1)S(1)} %bitcast.65) | data formatting | bytes 2211840 | tf_op jit(solution)/shard_map/reshape | solution.py:40
  25.5 0.0 copy-done
  25.5 1.6 %copy.25.grad = bf16[512,1440]{1,0:T(8,128)(2,1)} copy(bf16[512,1440]{0,1:T(8,128)(2,1)S(1)} %bitcast.63) | data formatting | bytes 2949120 | tf_op jit(solution)/shard_map/reshape | solution.py:293
  27.1 0.0 collective-permute-done.4
  27.1 4.5 %collective-permute-start = (bf16[2,1440,256]{2,1,0:T(8,128)(2,1)}, bf16[2,1440,256]{2,1,0:T(8,128)(2,1)}, u32[]{:S(2)}, u32[]{:S(2)}) collective-permute-start(bf16[2,1440,256]{2,1,0:T(8,128)(2,1)} %slice.72), channel_id=1, source_target_pairs={{0,1},{1,2},{2,3},{3,4},{4,5},{5,6},{6,7},{7,8},{8,9},{9,10},{10,1... | collective-permute-start | bytes 4423688 | tf_op jit(solution)/shard_map/ppermute | solution.py:23
  31.7 0.0 collective-permute-done.5
  31.7 1.2 convolution_convert_fusion.1
  33.0 1.5 reshape.64
  34.5 2.8 %copy.28 = bf16[10,64,9,48]{3,2,1,0:T(8,128)(2,1)} copy(bf16[10,64,9,48]{3,1,2,0:T(8,128)(2,1)S(1)} %bitcast.66) | data formatting | bytes 1105920 | tf_op jit(solution)/shard_map/reshape | solution.py:61
  37.3 4.3 %reshape.67.mats = bf16[640,432]{1,0:T(8,128)(2,1)} reshape(bf16[10,64,9,48]{3,2,1,0:T(8,128)(2,1)} %copy.28) | data formatting | bytes 1105920 | tf_op jit(solution)/shard_map/reshape | solution.py:61
  41.5 0.0 collective-permute-done.2
  41.6 0.0 collective-permute-done.3
  41.6 2.9 %fusion.grads = bf16[4,752,512]{2,1,0:T(8,128)(2,1)} fusion(bf16[1,720,512]{2,1,0:T(8,128)(2,1)} %collective-permute-done.3, bf16[2,720,512]{2,1,0:T(8,128)(2,1)S(1)} %bitcast.64, bf16[1,720,512]{2,1,0:T(8,128)(2,1)} %collective-permute-done.2), kind=kLoop, calls=%fused_computation.4 | loop fusion | flops 27721728 | bytes 6029312 | tf_op jit(solution)/shard_map/concatenate | solution.py:301
  44.5 0.0 collective-permute-done.1.above
  44.5 0.0 collective-permute-done.below
  44.5 22.9 %shard_map.94 = (bf16[1440,2304]{1,0:T(8,128)(2,1)}, f32[9,512,256]{2,1,0:T(8,128)}) custom-call(bf16[4,1440,256]{2,1,0:T(8,128)(2,1)} %bitcast.72, bf16[2,1440,256]{2,1,0:T(8,128)(2,1)} %collective-permute-done.below, bf16[1,1440,256]{2,1,0:T(8,128)(2,1)} %collective-permute-done.1.above, bf16[2,432,640]{2,1,0:T(8,128)(2,1)} %reshape.61.mats, ...), custom_call_target="tpu_custom_call" | custom-call | flops 10000000000 | bytes 7741440 | tf_op jit(solution)/shard_map/pallas_call | solution.py:252
  67.4 78.1 %shard_map.95 = (bf16[9,512,256]{2,1,0:T(8,128)(2,1)}, bf16[1440,512]{1,0:T(8,128)(2,1)}, bf16[4,1440,256]{2,1,0:T(8,128)(2,1)}) custom-call(f32[9,512,256]{2,1,0:T(8,128)} %get-tuple-element.8.term, bf16[1440,2304]{1,0:T(8,128)(2,1)} %get-tuple-element.9.inner, bf16[9,512,256]{2,1,0:T(8,128)(2,1)} %bitcast.75, bf16[4,752,512]{2,1,0:T(8,128)(2,1)} %fusion.grads, ...), custom_call_target="tpu_custom_call" | custom-call | flops 17999998976 | bytes 17346560 | tf_op jit(solution)/shard_map/pallas_call | solution.py:252
  145.6 0.0 copy-start.3
  145.6 4.4 %convert_bitcast_fusion = f32[512,9,256]{2,0,1:T(8,128)} fusion(bf16[9,512,256]{2,1,0:T(8,128)(2,1)} %get-tuple-element.12), kind=kLoop, calls=%fused_computation.1 | loop fusion | flops 1179648 | bytes 7077888 | tf_op jit(solution)/shard_map/transpose | solution.py:339
  150.0 0.0 copy-done.3
  150.0 0.0 copy-start.1
  150.0 1.1 copy.45
  151.1 1.3 copy-done.1
  152.4 1.6 %copy.46 = bf16[256,4,1440]{0,2,1:T(8,128)(2,1)} copy(bf16[256,4,1440]{0,2,1:T(8,128)(2,1)S(1)} %bitcast.70) | data formatting | bytes 5898240
  (15 shorter events, 0.1 us)
Async XLA Ops:
  2.1 29.6 %collective-permute-start.5 = (bf16[1,9,5,33]{3,1,2,0:T(8,128)(2,1)S(1)}, bf16[1,9,5,33]{3,1,2,0:T(8,128)(2,1)S(1)}, u32[]{:S(2)}, u32[]{:S(2)}) collective-permute-start(bf16[1,9,5,33]{3,1,2,0:T(8,128)(2,1)S(1)} %get-tuple-element.15), channel_id=1, source_target_pairs={{1,0},{2,1},{3,2},{4,3},{5,4},{6,5},{7,6},{8,7},{9,8},{10,9},{11,1... | collective-permute-start | bytes 8918 | tf_op jit(solution)/shard_map/ppermute | solution.py:23
  3.4 23.6 %collective-permute-start.4 = (bf16[1,9,5,33]{3,1,2,0:T(8,128)(2,1)S(1)}, bf16[1,9,5,33]{3,1,2,0:T(8,128)(2,1)S(1)}, u32[]{:S(2)}, u32[]{:S(2)}) collective-permute-start(bf16[1,9,5,33]{3,1,2,0:T(8,128)(2,1)S(1)} %get-tuple-element.16), channel_id=1, source_target_pairs={{0,1},{1,2},{2,3},{3,4},{4,5},{5,6},{6,7},{7,8},{8,9},{9,10},{10,1... | collective-permute-start | bytes 8918 | tf_op jit(solution)/shard_map/ppermute | solution.py:23
  6.5 14.9 %copy-start.2 = (bf16[256,4,1440]{0,2,1:T(8,128)(2,1)S(1)}, bf16[256,4,1440]{0,2,1:T(8,128)(2,1)}, u32[]{:S(2)}) copy-start(bf16[256,4,1440]{0,2,1:T(8,128)(2,1)} %param.7) | copy-start | bytes 8847364
  8.7 35.8 %collective-permute-start.1 = (bf16[1,1440,256]{2,1,0:T(8,128)(2,1)}, bf16[1,1440,256]{2,1,0:T(8,128)(2,1)}, u32[]{:S(2)}, u32[]{:S(2)}) collective-permute-start(bf16[1,1440,256]{2,1,0:T(8,128)(2,1)} %slice.73), channel_id=1, source_target_pairs={{1,0},{2,1},{3,2},{4,3},{5,4},{6,5},{7,6},{8,7},{9,8},{10,9},{11,1... | collective-permute-start | bytes 2211848 | tf_op jit(solution)/shard_map/ppermute | solution.py:23
  12.5 29.0 %collective-permute-start.2 = (bf16[1,720,512]{2,1,0:T(8,128)(2,1)}, bf16[1,720,512]{2,1,0:T(8,128)(2,1)}, u32[]{:S(2)}, u32[]{:S(2)}) collective-permute-start(bf16[1,720,512]{2,1,0:T(8,128)(2,1)} %get-tuple-element.13), channel_id=1, source_target_pairs={{0,1},{1,2},{2,3},{3,4},{4,5},{5,6},{6,7},{7,8},{8,9},{9,10},{10,1... | collective-permute-start | bytes 2211848 | tf_op jit(solution)/shard_map/ppermute | solution.py:23
  18.5 23.0 %collective-permute-start.3 = (bf16[1,720,512]{2,1,0:T(8,128)(2,1)}, bf16[1,720,512]{2,1,0:T(8,128)(2,1)}, u32[]{:S(2)}, u32[]{:S(2)}) collective-permute-start(bf16[1,720,512]{2,1,0:T(8,128)(2,1)} %get-tuple-element.14), channel_id=1, source_target_pairs={{1,0},{2,1},{3,2},{4,3},{5,4},{6,5},{7,6},{8,7},{9,8},{10,9},{11,1... | collective-permute-start | bytes 2211848 | tf_op jit(solution)/shard_map/ppermute | solution.py:23
  22.9 2.6 %copy-start = (bf16[512,2,720]{0,2,1:T(8,128)(2,1)S(1)}, bf16[512,2,720]{0,2,1:T(8,128)(2,1)}, u32[]{:S(2)}) copy-start(bf16[512,2,720]{0,2,1:T(8,128)(2,1)} %param.11) | copy-start | bytes 4423684
  27.1 17.4 %collective-permute-start = (bf16[2,1440,256]{2,1,0:T(8,128)(2,1)}, bf16[2,1440,256]{2,1,0:T(8,128)(2,1)}, u32[]{:S(2)}, u32[]{:S(2)}) collective-permute-start(bf16[2,1440,256]{2,1,0:T(8,128)(2,1)} %slice.72), channel_id=1, source_target_pairs={{0,1},{1,2},{2,3},{3,4},{4,5},{5,6},{6,7},{7,8},{8,9},{9,10},{10,1... | collective-permute-start | bytes 4423688 | tf_op jit(solution)/shard_map/ppermute | solution.py:23
  145.6 4.4 %copy-start.3 = (bf16[1440,512]{1,0:T(8,128)(2,1)S(1)}, bf16[1440,512]{1,0:T(8,128)(2,1)}, u32[]{:S(2)}) copy-start(bf16[1440,512]{1,0:T(8,128)(2,1)} %get-tuple-element.10) | copy-start | bytes 4423684
  150.0 2.4 %copy-start.1 = (bf16[4,1440,256]{2,1,0:T(8,128)(2,1)S(1)}, bf16[4,1440,256]{2,1,0:T(8,128)(2,1)}, u32[]{:S(2)}) copy-start(bf16[4,1440,256]{2,1,0:T(8,128)(2,1)} %get-tuple-element.11) | copy-start | bytes 8847364

commit v3 on v2

--- a/solution.py
+++ b/solution.py
@@ -21,6 +21,15 @@
     size = lax.axis_size(axis)
     pairs = [(i, i + by) for i in range(size) if 0 <= i + by < size]
     return lax.ppermute(shard, axis, pairs)
+
+
+def together(grads, masked, by):
+    length, outs = grads.shape[1:]
+    flat = masked.reshape(1, -1, masked.shape[3])
+    depth, taps = flat.shape[1:]
+    extra = jnp.pad(flat, ((0, 0), (0, -depth % 16), (0, outs - taps)))
+    got = shifted(jnp.concatenate([grads, extra], 1), "lat", by)
+    return got[:, :length], got[:, length : length + depth, :taps].reshape(masked.shape)
 
 
 def masked_basis(filter_basis, halo_reach):
@@ -103,11 +112,12 @@
     steps = size.bit_length() - 1
     outs, chans = term.shape[1:]
     me = lax.axis_index("lat")
-    bits = [lax.rem(me // (1 << s), 2) for s in range(steps)]
-    partners = [me + (1 - 2 * bits[s]) * (1 << s) for s in range(steps)]
+    orders = [list(range(steps)), [0, *range(2, steps), 1][:steps]]
+    bit_of = [lax.rem(me // (1 << s), 2) for s in range(steps)]
+    partner_of = [me + (1 - 2 * bit_of[s]) * (1 << s) for s in range(steps)]
     halves = [outs >> (s + 1) for s in range(steps)]
     barrier = pltpu.get_barrier_semaphore()
-    for partner in partners:
+    for partner in partner_of:
         pl.semaphore_signal(
             barrier, inc=1, device_id={"lat": partner}, device_id_type=pl.DeviceIdType.MESH
         )
@@ -116,8 +126,11 @@
     cut = (kernels + 1) // 2
     chunks = [slice(0, cut), slice(cut, kernels)]
 
-    def place(first, s):
-        return sum((bits[t] * halves[t] for t in range(first, s)), 0 * me)
+    def bit(c, s):
+        return bit_of[orders[c][s]]
+
+    def place(c, first, s):
+        return sum((bit(c, t) * halves[t] for t in range(first, s)), 0 * me)
 
     def rows(start, count):
         return pl.ds(pl.multiple_of(start, 16), count)
@@ -128,7 +141,7 @@
             dst_ref=target,
             send_sem=send_sem.at[c, t],
             recv_sem=recv_sem.at[c, t],
-            device_id={"lat": partners[s]},
+            device_id={"lat": partner_of[orders[c][s]]},
             device_id_type=pl.DeviceIdType.MESH,
         )
         made.start()
@@ -139,14 +152,15 @@
         if t < steps:
             h, lag = halves[t], outs - (outs >> t)
             source = term if t == 0 else acc
-            away = rows(place(1, t) + (1 - bits[t]) * h, h)
+            away = rows(place(c, 1, t) + (1 - bit(c, t)) * h, h)
             sent[ks, lag : lag + h] = source[ks, away].astype(BF16)
             return copy(c, t, sent.at[ks, lag : lag + h], got.at[ks, lag : lag + h], t)
         s = 2 * steps - 1 - t
         if t == steps:
             last = halves[-1]
-            weight[ks, rows(place(0, steps), last)] = acc[ks, rows(place(1, steps), last)].astype(BF16)
-        mine = weight.at[ks, rows(place(0, s + 1), halves[s])]
+            own = acc[ks, rows(place(c, 1, steps), last)]
+            weight[ks, rows(place(c, 0, steps), last)] = own.astype(BF16)
+        mine = weight.at[ks, rows(place(c, 0, s + 1), halves[s])]
         return copy(c, t, mine, mine, s)
 
     def finish(c, t, made):
@@ -155,7 +169,7 @@
         if t < steps:
             h, lag = halves[t], outs - (outs >> t)
             arrived = got[ks, lag : lag + h].astype(F32)
-            at = rows(place(1, t) + bits[t] * h, h)
+            at = rows(place(c, 1, t) + bit(c, t) * h, h)
             if t == 0:
                 acc[ks] = term[ks, at] + arrived
             else:
@@ -272,11 +286,9 @@
     below = shifted(own[rows_own - 2 :], "lat", 1)
     above = shifted(own[:1], "lat", -1)
     grads = grad_out.transpose(1, 2, 0)
-    grad_below = shifted(grads[count - 1 :], "lat", 1)
-    grad_above = shifted(grads[:1], "lat", -1)
     masked = masked_basis(filter_basis, halo_reach)
-    masked_below = shifted(masked[count - 1 :], "lat", 1)
-    masked_above = shifted(masked[:1], "lat", -1)
+    grad_below, masked_below = together(grads[count - 1 :], masked[count - 1 :], 1)
+    grad_above, masked_above = together(grads[:1], masked[:1], -1)
     mixer = filter_weight.transpose(1, 0, 2)
 
     factor = 1.0 / math.sqrt(lax.axis_size("lat") * count * out_width)

time: 154 us -> 148 us (0.961)
  starting transfers between devices: 17.4 us -> 12 us
  local copies, waits for them, and re-layouts: 23.1 us -> 25.7 us
  Pallas kernels: 101 us -> 99 us
  matrix products: 2.75 us -> 0.76 us
    ppermute x6 -> x4, starting transfers between devices: 17.4 us -> 12 us  [shifted(): return lax.ppermute(shard, axis, pairs)]
    slice x2 -> x10, local copies, waits for them, and re-layouts: 2.56 us -> 5.23 us  [the longest x2 2.33 us: together(): got[:, :length]]
    pallas_call x2, Pallas kernels: 101 us -> 99 us  [call(): pl.pallas_call(body, out_shape=out_shape, in_specs=[whole] * len(args), o...]
    concatenate x0 -> x2, other arithmetic: none -> 1.86 us  [together(): got = shifted(jnp.concatenate([grads, extra], 1), 'lat', by)]
    unnamed x21 -> x25, local copies, waits for them, and re-layouts: 4.34 us -> 4.36 us
  transfers between devices with their start and end apart: 6 -> 4, of which waited for: 0 -> 0; matrix products, arithmetic and copies ran while one was open for 16% -> 16% of each run, Pallas kernels for 0% -> 0%
where the time goes in v3:
time: 148 us
  Pallas kernels  99 us (67%)
  local copies, waits for them, and re-layouts  25.7 us (17%)
  starting transfers between devices  12 us (8%)
  other arithmetic  9.54 us (6%)
    pallas_call x2, Pallas kernels, call(): pl.pallas_call(body, out_shape=out_shape, in_specs=[whole] * len(args), o...  99 us
    ppermute x4, starting transfers between devices, shifted(): return lax.ppermute(shard, axis, pairs)  12 us
    reshape x2, local copies, waits for them, and re-layouts, backward_matrix(): return spread.reshape(len(pairs) * 2 * BACK_BLOCK, kernels * span)  7.05 us
    transpose x1, other arithmetic, on_device(): grad_weight.transpose(1, 0, 2)  4.41 us
    unnamed x25, local copies, waits for them, and re-layouts  4.36 us
  transfers between devices with their start and end apart: 4, of which 0 were waited for; matrix products, arithmetic and copies ran while one was open for 16% of the time, Pallas kernels for 0%

profile of v3, /device:TPU:0, one launch (start us, length us, event | category | flops | bytes accessed | tf_op | source)
XLA Modules:
  0.0 147.9 jit_solution(15777281032456890405)
XLA Ops:
  0.6 0.7 compare_convert_fusion
  1.4 0.7 copy_multiply_fusion
  2.2 1.4 fusion.6
  3.6 0.9 fusion.5
  4.5 1.3 collective-permute-start.3
  5.9 0.0 copy-start.2
  5.9 0.0 copy-start.4
  5.9 0.9 fusion.4
  6.8 4.1 %collective-permute-start.2 = (bf16[1,768,512]{2,1,0:T(8,128)(2,1)}, bf16[1,768,512]{2,1,0:T(8,128)(2,1)}, u32[]{:S(2)}, u32[]{:S(2)}) collective-permute-start(bf16[1,768,512]{2,1,0:T(8,128)(2,1)} %fusion.4), channel_id=1, source_target_pairs={{0,1},{1,2},{2,3},{3,4},{4,5},{5,6},{6,7},{7,8},{8,9},{9,10},{10,1... | collective-permute-start | bytes 2359304 | tf_op jit(solution)/shard_map/ppermute | solution.py:23
  10.9 2.0 %slice.89 = bf16[1,1440,256]{2,1,0:T(8,128)(2,1)} slice(bf16[4,1440,256]{2,1,0:T(8,128)(2,1)} %bitcast.69), slice={[0:1], [0:1440], [0:256]} | slice | bytes 1474560 | tf_op jit(solution)/shard_map/slice | solution.py:287
  12.9 1.3 collective-permute-start.1
  14.2 0.0 copy-done.2
  14.2 1.2 slice.88
  15.4 5.3 %collective-permute-start = (bf16[2,1440,256]{2,1,0:T(8,128)(2,1)}, bf16[2,1440,256]{2,1,0:T(8,128)(2,1)}, u32[]{:S(2)}, u32[]{:S(2)}) collective-permute-start(bf16[2,1440,256]{2,1,0:T(8,128)(2,1)} %slice.88), channel_id=1, source_target_pairs={{0,1},{1,2},{2,3},{3,4},{4,5},{5,6},{6,7},{7,8},{8,9},{9,10},{10,1... | collective-permute-start | bytes 4423688 | tf_op jit(solution)/shard_map/ppermute | solution.py:23
  20.8 0.0 copy-done.4
  20.8 0.5 convolution_convert_fusion
  21.3 0.2 copy.47
  21.5 0.1 slice.108
  21.6 0.0 copy-start
  21.6 0.5 copy.57
  22.1 2.1 %reshape.73.mats = bf16[2,432,640]{2,1,0:T(8,128)(2,1)} reshape(bf16[2,9,48,5,128]{4,3,2,1,0:T(8,128)(2,1)S(1)} %bitcast.63) | data formatting | bytes 2211840 | tf_op jit(solution)/shard_map/reshape | solution.py:49
  24.2 0.0 copy-start.5
  24.2 0.0 copy-done
  24.2 1.6 %copy.35.grad = bf16[512,1440]{1,0:T(8,128)(2,1)} copy(bf16[512,1440]{0,1:T(8,128)(2,1)S(1)} %bitcast.61) | data formatting | bytes 2949120 | tf_op jit(solution)/shard_map/reshape | solution.py:305
  25.8 0.0 collective-permute-done.3
  25.8 0.7 slice.105
  26.5 0.0 collective-permute-done.2
  26.5 0.7 slice.96
  27.4 0.0 copy-done.5
  27.5 0.3 convolution_convert_fusion.1
  27.8 1.5 %reshape.80 = bf16[10,9,64,48]{3,2,1,0:T(8,128)(2,1)S(1)} reshape(bf16[90,3072]{1,0:T(8,128)(2,1)S(1)} %convolution_convert_fusion.1) | data formatting | bytes 1105920 | tf_op jit(solution)/shard_map/reshape | solution.py:69
  29.3 2.8 %copy.42 = bf16[10,64,9,48]{3,2,1,0:T(8,128)(2,1)} copy(bf16[10,64,9,48]{3,1,2,0:T(8,128)(2,1)S(1)} %bitcast.64) | data formatting | bytes 1105920 | tf_op jit(solution)/shard_map/reshape | solution.py:70
  32.0 4.3 %reshape.83.mats = bf16[640,432]{1,0:T(8,128)(2,1)} reshape(bf16[10,64,9,48]{3,2,1,0:T(8,128)(2,1)} %copy.42) | data formatting | bytes 1105920 | tf_op jit(solution)/shard_map/reshape | solution.py:70
  36.3 1.2 slice.95
  37.5 1.2 slice.92
  38.6 1.8 %fusion.grads = bf16[4,752,512]{2,1,0:T(8,128)(2,1)} fusion(bf16[1,720,512]{2,1,0:T(8,128)(2,1)S(1)} %slice.95, bf16[2,720,512]{2,1,0:T(8,128)(2,1)S(1)} %bitcast.62, bf16[1,720,512]{2,1,0:T(8,128)(2,1)S(1)} %slice.92), kind=kLoop, calls=%fused_computation.4 | loop fusion | flops 27721728 | bytes 6029312 | tf_op jit(solution)/shard_map/concatenate | solution.py:313
  40.4 0.0 collective-permute-done.1.above
  40.4 0.0 collective-permute-done.below
  40.4 22.9 %shard_map.94 = (bf16[1440,2304]{1,0:T(8,128)(2,1)}, f32[9,512,256]{2,1,0:T(8,128)}) custom-call(bf16[4,1440,256]{2,1,0:T(8,128)(2,1)} %bitcast.70, bf16[2,1440,256]{2,1,0:T(8,128)(2,1)} %collective-permute-done.below, bf16[1,1440,256]{2,1,0:T(8,128)(2,1)} %collective-permute-done.1.above, bf16[2,432,640]{2,1,0:T(8,128)(2,1)} %reshape.73.mats, ...), custom_call_target="tpu_custom_call" | custom-call | flops 10000000000 | bytes 7741440 | tf_op jit(solution)/shard_map/pallas_call | solution.py:266
  63.4 76.1 %shard_map.95 = (bf16[9,512,256]{2,1,0:T(8,128)(2,1)}, bf16[1440,512]{1,0:T(8,128)(2,1)}, bf16[4,1440,256]{2,1,0:T(8,128)(2,1)}) custom-call(f32[9,512,256]{2,1,0:T(8,128)} %get-tuple-element.8.term, bf16[1440,2304]{1,0:T(8,128)(2,1)} %get-tuple-element.9.inner, bf16[9,512,256]{2,1,0:T(8,128)(2,1)} %bitcast.73, bf16[4,752,512]{2,1,0:T(8,128)(2,1)} %fusion.grads, ...), custom_call_target="tpu_custom_call" | custom-call | flops 17999998976 | bytes 17346560 | tf_op jit(solution)/shard_map/pallas_call | solution.py:266
  139.5 0.0 copy-start.3
  139.5 4.4 %convert_bitcast_fusion = f32[512,9,256]{2,0,1:T(8,128)} fusion(bf16[9,512,256]{2,1,0:T(8,128)(2,1)} %get-tuple-element.12), kind=kLoop, calls=%fused_computation.1 | loop fusion | flops 1179648 | bytes 7077888 | tf_op jit(solution)/shard_map/transpose | solution.py:351
  143.9 0.0 copy-done.3
  143.9 0.0 copy-start.1
  143.9 1.1 copy.69
  145.0 1.3 copy-done.1
  146.3 1.6 %copy.70 = bf16[256,4,1440]{0,2,1:T(8,128)(2,1)} copy(bf16[256,4,1440]{0,2,1:T(8,128)(2,1)S(1)} %bitcast.68) | data formatting | bytes 5898240
  (23 shorter events, 0.3 us)
Async XLA Ops:
  4.5 21.3 %collective-permute-start.3 = (bf16[1,768,512]{2,1,0:T(8,128)(2,1)}, bf16[1,768,512]{2,1,0:T(8,128)(2,1)}, u32[]{:S(2)}, u32[]{:S(2)}) collective-permute-start(bf16[1,768,512]{2,1,0:T(8,128)(2,1)} %fusion.5), channel_id=1, source_target_pairs={{1,0},{2,1},{3,2},{4,3},{5,4},{6,5},{7,6},{8,7},{9,8},{10,9},{11,1... | collective-permute-start | bytes 2359304 | tf_op jit(solution)/shard_map/ppermute | solution.py:23
  5.9 8.4 %copy-start.2 = (bf16[256,4,1440]{0,2,1:T(8,128)(2,1)S(1)}, bf16[256,4,1440]{0,2,1:T(8,128)(2,1)}, u32[]{:S(2)}) copy-start(bf16[256,4,1440]{0,2,1:T(8,128)(2,1)} %param.7) | copy-start | bytes 8847364
  5.9 14.9 %copy-start.4 = (bf16[33,6144]{1,0:T(8,128)(2,1)S(1)}, bf16[33,6144]{1,0:T(8,128)(2,1)}, u32[]{:S(2)}) copy-start(bf16[33,6144]{1,0:T(8,128)(2,1)} %constant.10.clone) | copy-start | bytes 1216516
  6.8 19.7 %collective-permute-start.2 = (bf16[1,768,512]{2,1,0:T(8,128)(2,1)}, bf16[1,768,512]{2,1,0:T(8,128)(2,1)}, u32[]{:S(2)}, u32[]{:S(2)}) collective-permute-start(bf16[1,768,512]{2,1,0:T(8,128)(2,1)} %fusion.4), channel_id=1, source_target_pairs={{0,1},{1,2},{2,3},{3,4},{4,5},{5,6},{6,7},{7,8},{8,9},{9,10},{10,1... | collective-permute-start | bytes 2359304 | tf_op jit(solution)/shard_map/ppermute | solution.py:23
  12.9 27.5 %collective-permute-start.1 = (bf16[1,1440,256]{2,1,0:T(8,128)(2,1)}, bf16[1,1440,256]{2,1,0:T(8,128)(2,1)}, u32[]{:S(2)}, u32[]{:S(2)}) collective-permute-start(bf16[1,1440,256]{2,1,0:T(8,128)(2,1)} %slice.89), channel_id=1, source_target_pairs={{1,0},{2,1},{3,2},{4,3},{5,4},{6,5},{7,6},{8,7},{9,8},{10,9},{11,1... | collective-permute-start | bytes 2211848 | tf_op jit(solution)/shard_map/ppermute | solution.py:23
  15.4 25.0 %collective-permute-start = (bf16[2,1440,256]{2,1,0:T(8,128)(2,1)}, bf16[2,1440,256]{2,1,0:T(8,128)(2,1)}, u32[]{:S(2)}, u32[]{:S(2)}) collective-permute-start(bf16[2,1440,256]{2,1,0:T(8,128)(2,1)} %slice.88), channel_id=1, source_target_pairs={{0,1},{1,2},{2,3},{3,4},{4,5},{5,6},{6,7},{7,8},{8,9},{9,10},{10,1... | collective-permute-start | bytes 4423688 | tf_op jit(solution)/shard_map/ppermute | solution.py:23
  21.6 2.6 %copy-start = (bf16[512,2,720]{0,2,1:T(8,128)(2,1)S(1)}, bf16[512,2,720]{0,2,1:T(8,128)(2,1)}, u32[]{:S(2)}) copy-start(bf16[512,2,720]{0,2,1:T(8,128)(2,1)} %param.11) | copy-start | bytes 4423684
  24.2 3.2 %copy-start.5 = (bf16[33,3072]{1,0:T(8,128)(2,1)S(1)}, bf16[33,3072]{1,0:T(8,128)(2,1)}, u32[]{:S(2)}) copy-start(bf16[33,3072]{1,0:T(8,128)(2,1)} %constant.11.clone) | copy-start | bytes 608260
  139.5 4.4 %copy-start.3 = (bf16[1440,512]{1,0:T(8,128)(2,1)S(1)}, bf16[1440,512]{1,0:T(8,128)(2,1)}, u32[]{:S(2)}) copy-start(bf16[1440,512]{1,0:T(8,128)(2,1)} %get-tuple-element.10) | copy-start | bytes 4423684
  143.9 2.4 %copy-start.1 = (bf16[4,1440,256]{2,1,0:T(8,128)(2,1)S(1)}, bf16[4,1440,256]{2,1,0:T(8,128)(2,1)}, u32[]{:S(2)}) copy-start(bf16[4,1440,256]{2,1,0:T(8,128)(2,1)} %get-tuple-element.11) | copy-start | bytes 8847364
